TPU v7x, 128 devices: a whole 4x4x4 slice. The times are simulated.
128 devices in a mesh: rep: 16 (over y_lo, z, core), tp: 8 (over y_hi, x).
Axes of the slice: x: 4, y: 4 (y_hi: 2, y_lo: 2; y = y_hi * 2 + y_lo), z: 4, core: 2. Of those that a mesh axis runs over, the one named last changes fastest.
Arguments:
- queries: bfloat16 [512, 8192], P('rep', 'tp'), may hold values from -5.5 to 5.5
- new_token_kv: bfloat16 [512, 2048], P('rep', 'tp'), may hold values from -5 to 5
- resident_cache: bfloat16 [512, 384, 2048], P('rep', None, 'tp'), may hold values from -5.5 to 5.5
- resident_lengths: int32 [16, 32], P('rep'), may hold values from 1 to 383, 7660 in all within a row
- new_caches: bfloat16 [256, 8, 128, 512], P('rep', 'tp'), may hold values from -5.5 to 5.5
- new_lengths: int32 [16, 16], P('rep'), may hold values from 1 to 256, 2560 in all within a row
- handoff: int32 [16, 16, 2], P('rep'), may hold values from 0 to 31, as said below
- out_weight: bfloat16 [8192, 8192], P('tp'), may hold values from -0.1875 to 0.1875
Outputs:
- attended: bfloat16 [512, 8192], P('rep')
- updated_cache: bfloat16 [512, 384, 2048], P('rep', None, 'tp')
Inputs may be any that keep to these rules, and one draw needn't show every extreme that they name: handoff[g, i] = (decode group, row) of request i of group g. No group hands more than 2 requests to one decode group; one decode group receives exactly 2 from every group; the rows named for one decode group are distinct.
All inputs are finite; a program needn't handle non-finite values.
Results may differ from a plain program's by a relative error of at most 0.008.
Values may be sent and summed in bfloat16 or wider, within the bound.
A program may use at most 128 MiB of HBM per device.

v0:
```python
import jax
import jax.numpy as jnp
from jax import lax
from jax.sharding import PartitionSpec as P

HEAD = 128
CAP = 2


NEG_FILL = -1e30


def from_partner(array, axis, bit):
    return lax.ppermute(array, axis, [(i, i ^ 1 << bit) for i in range(lax.axis_size(axis))])


def partial_softmax(query_rows, key_rows, value_rows, valid_mask):
    scores = jnp.einsum(
        "nkgd,nlkd->nkgl", query_rows, key_rows, preferred_element_type=jnp.float32
    ) * HEAD ** (-0.5)
    allowed = valid_mask[:, None, None, :]
    maxima = jnp.max(jnp.where(allowed, scores, NEG_FILL), axis=3)
    shifted = jnp.where(allowed, scores, maxima[..., None]) - maxima[..., None]
    exp_scores = jnp.where(allowed, jnp.exp(shifted), 0.0)
    weights = exp_scores.astype(jnp.bfloat16)
    totals = jnp.sum(weights.astype(jnp.float32), axis=3)
    accumulated = jnp.einsum(
        "nkgl,nlkd->nkgd", weights, value_rows, preferred_element_type=jnp.float32
    )
    return (maxima, totals, accumulated)


def combine_partials(pieces_list, own_score, own_value):
    running_peak = own_score
    for maxima, totals, accumulated in pieces_list:
        running_peak = jnp.maximum(running_peak, maxima)
    own_weight = jnp.exp(own_score - running_peak)
    numerator = own_weight[..., None] * own_value[:, :, None, :]
    denominator = own_weight
    for maxima, totals, accumulated in pieces_list:
        factor = jnp.exp(maxima - running_peak)
        numerator = numerator + factor[..., None] * accumulated
        denominator = denominator + factor * totals
    return numerator / denominator[..., None]


def take_halves(full_heads, query_rows, lengths_of, half_len):
    entry_count = full_heads.shape[0]
    cache_view = full_heads.reshape(entry_count, 2 * half_len, -1, 2, HEAD)
    offsets = jnp.arange(half_len, dtype=jnp.int32)
    lower_part = partial_softmax(
        query_rows,
        cache_view[:, :half_len, :, 0, :],
        cache_view[:, :half_len, :, 1, :],
        offsets[None, :] < lengths_of[:, None],
    )
    upper_part = partial_softmax(
        query_rows,
        cache_view[:, half_len:, :, 0, :],
        cache_view[:, half_len:, :, 1, :],
        (offsets + half_len)[None, :] < lengths_of[:, None],
    )
    return [lower_part, upper_part]


def body(
    queries,
    new_token_kv,
    resident_cache,
    resident_lengths,
    new_caches,
    new_lengths,
    handoff,
    out_weight,
):
    row_count = queries.shape[0]
    cache_len = resident_cache.shape[1]
    piece_width = resident_cache.shape[2]
    kv_here = piece_width // (2 * HEAD)
    per_kv = queries.shape[1] // (HEAD * kv_here)
    half_len = new_caches.shape[2]
    group_count = lax.axis_size("rep")
    entries = group_count * CAP
    parity = lax.axis_index("tp") % 2
    query_rows = queries.reshape(row_count, kv_here, per_kv, HEAD)
    own_view = new_token_kv.reshape(row_count, kv_here, 2, HEAD)
    own_score = jnp.einsum(
        "nkgd,nkd->nkg", query_rows, own_view[:, :, 0, :], preferred_element_type=jnp.float32
    ) * HEAD ** (-0.5)
    own_value = own_view[:, :, 1, :].astype(jnp.float32)
    lengths_here = resident_lengths[0]
    positions = jnp.arange(cache_len, dtype=jnp.int32)
    cache_view = resident_cache.reshape(row_count, cache_len, kv_here, 2, HEAD)
    resident_part = partial_softmax(
        query_rows,
        cache_view[:, :, :, 0, :],
        cache_view[:, :, :, 1, :],
        positions[None, :] < lengths_here[:, None],
    )
    resident_out = combine_partials([resident_part], own_score, own_value)
    dest_group = handoff[0, :, 0]
    dest_row = handoff[0, :, 1]
    request_lengths = new_lengths[0]
    request_count = dest_group.shape[0]
    request_ids = jnp.arange(request_count, dtype=jnp.int32)
    earlier = (dest_group[:, None] == dest_group[None, :]) & (
        request_ids[None, :] < request_ids[:, None]
    )
    slot_index = dest_group * CAP + jnp.sum(earlier.astype(jnp.int32), axis=1)
    matches = slot_index[None, :] == jnp.arange(entries, dtype=jnp.int32)[:, None]
    filled = jnp.any(matches, axis=1)
    source = jnp.sum(jnp.where(matches, request_ids[None, :], 0), axis=1)
    metadata = jnp.stack(
        [jnp.where(filled, dest_row[source], -1), jnp.where(filled, request_lengths[source], 0)],
        axis=1,
    )
    metadata = metadata.reshape(group_count, CAP, 2)
    prefill_pieces = new_caches[:, 0]
    packed = jnp.where(
        filled[:, None, None], prefill_pieces[source], jnp.zeros((), prefill_pieces.dtype)
    )
    packed = packed.reshape(group_count, CAP, prefill_pieces.shape[1], prefill_pieces.shape[2])
    buffer = lax.all_to_all(packed, "rep", split_axis=0, concat_axis=0, tiled=True)
    incoming = lax.all_to_all(metadata, "rep", split_axis=0, concat_axis=0, tiled=True)
    sources = buffer.shape[0]
    item_count = buffer.shape[1]
    entry_count = sources * item_count
    flattened = buffer.reshape(entry_count, buffer.shape[2], buffer.shape[3])
    incoming = incoming.reshape(entry_count, 2)
    rows_of = incoming[:, 0]
    lengths_of = incoming[:, 1]
    selector = (rows_of[:, None] == jnp.arange(row_count, dtype=jnp.int32)[None, :]).astype(
        jnp.bfloat16
    )
    entry_queries = jnp.dot(selector, queries, preferred_element_type=jnp.float32).astype(
        jnp.bfloat16
    )
    entry_queries = entry_queries.reshape(entry_count, kv_here, per_kv, HEAD)
    entry_own = jnp.dot(selector, new_token_kv, preferred_element_type=jnp.float32).astype(
        jnp.bfloat16
    )
    entry_own = entry_own.reshape(entry_count, kv_here, 2, HEAD)
    entry_score = jnp.einsum(
        "nkgd,nkd->nkg", entry_queries, entry_own[:, :, 0, :], preferred_element_type=jnp.float32
    ) * HEAD ** (-0.5)
    entry_value = entry_own[:, :, 1, :].astype(jnp.float32)
    own_piece = lax.dynamic_slice_in_dim(flattened, parity * piece_width, piece_width, 2)
    theirs = lax.dynamic_slice_in_dim(flattened, (1 - parity) * piece_width, piece_width, 2)
    partner_half = from_partner(theirs, "tp", 0)
    full_heads = jnp.concatenate(
        [
            jnp.where(parity == 0, own_piece, partner_half),
            jnp.where(parity == 0, partner_half, own_piece),
        ],
        axis=1,
    )
    pieces_list = take_halves(full_heads, entry_queries, lengths_of, half_len)
    entry_out = combine_partials(pieces_list, entry_score, entry_value)
    entry_out, full_heads, incoming = (
        entry_out.reshape(sources, item_count, -1),
        full_heads.reshape(sources, item_count, 2 * half_len, piece_width),
        incoming.reshape(sources, item_count, 2),
    )
    entry_out = entry_out.reshape(entries, -1)
    full_heads = full_heads.reshape(entries, 2 * half_len, piece_width)
    incoming = incoming.reshape(entries, 2)
    matches_rows = incoming[:, 0][:, None] == jnp.arange(row_count, dtype=jnp.int32)[None, :]
    replaced = jnp.any(matches_rows, axis=0)
    entry_index = jnp.sum(
        jnp.where(matches_rows, jnp.arange(entries, dtype=jnp.int32)[:, None], 0), axis=0
    )
    arrived_out = entry_out[entry_index]
    attention_rows = jnp.where(
        replaced[:, None], arrived_out, resident_out.reshape(row_count, -1)
    ).astype(jnp.bfloat16)
    head_terms = jnp.dot(attention_rows, out_weight, preferred_element_type=jnp.float32)
    attended = lax.psum(head_terms, "tp").astype(jnp.bfloat16)
    arrived_len = jnp.where(replaced, incoming[entry_index, 1], 0)
    padded = jnp.pad(full_heads[entry_index], ((0, 0), (0, cache_len - 2 * half_len), (0, 0)))
    slot_ids = positions[None, :, None]
    own_flat = new_token_kv[:, None, :]
    installed = jnp.where(
        slot_ids == arrived_len[:, None, None],
        own_flat,
        jnp.where(slot_ids < arrived_len[:, None, None], padded, jnp.zeros((), padded.dtype)),
    )
    resident_kept = jnp.where(slot_ids == lengths_here[:, None, None], own_flat, resident_cache)
    updated = jnp.where(replaced[:, None, None], installed, resident_kept)
    return (attended, updated)


def solution(mesh):
    placed = (
        P("rep", "tp"),
        P("rep", "tp"),
        P("rep", None, "tp"),
        P("rep", None),
        P("rep", "tp", None, None),
        P("rep", None),
        P("rep", None, None),
        P("tp", None),
    )
    return jax.shard_map(
        body,
        mesh=mesh,
        in_specs=placed,
        out_specs=(P("rep", None), P("rep", None, "tp")),
        check_vma=False,
    )
```

profile of v0, /device:TPU:96, one launch (start us, length us, event | category | flops | bytes accessed | tf_op | source)
XLA Modules:
  0.0 258.9 jit_solution(11352044058149583983)
XLA Ops:
  0.6 0.0 copy-start
  0.6 0.8 slice_bitcast_fusion.24
  1.5 0.2 convert_reduce_fusion.3
  1.7 0.7 multiply_add_fusion.2
  2.4 0.1 select_reduce_fusion.4
  2.5 0.1 fusion.22
  2.6 0.7 gather_fusion
  3.3 1.4 gather_fusion.1
  4.6 0.1 select_n.160
  4.7 0.1 select_n.162
  4.8 0.6 copy.42
  5.4 5.5 %all-to-all-start = ((s32[16,2,2]{1,2,0:T(2,128)}), s32[16,2,2]{1,2,0:T(2,128)S(1)}, u32[]{:S(2)}, u32[]{:S(2)}) async-start(s32[16,2,2]{1,2,0:T(2,128)} %copy.42), calls=%async_computation | async-start | bytes 32768 | tf_op jit(solution)/shard_map/all_to_all | solution.py:124
  11.0 0.1 broadcast_in_dim.226
  11.1 0.0 copy-done
  11.1 2.8 %gather_fusion.2 = bf16[32,128,512]{2,1,0:T(8,128)(2,1)} fusion(bf16[16,128,512]{2,1,0:T(8,128)(2,1)S(1)} %bitcast.108, s32[1024]{0:T(1024)S(1)} %pad_clamp_fusion.1), kind=kCustom, calls=%fused_computation.2 | custom fusion | bytes 8388736 | tf_op jit(solution)/shard_map/gather | solution.py:120
  13.9 4.5 %broadcast_select_fusion = bf16[16,2,128,512]{3,2,1,0:T(8,128)(2,1)} fusion(bf16[16,2,128,512]{3,2,1,0:T(8,128)(2,1)} %bitcast.110, pred[16,2]{1,0:T(8,128)(4,1)S(1)} %broadcast_in_dim.226), kind=kLoop, calls=%fused_computation.8 | loop fusion | flops 2097152 | bytes 8388640 | tf_op jit(solution)/shard_map/jit(_where)/select_n | solution.py:119
  18.4 0.0 all-to-all-done
  18.4 5.7 %all-to-all-start.1 = ((bf16[16,2,128,512]{3,2,1,0:T(8,128)(2,1)}), bf16[16,2,128,512]{3,2,1,0:T(8,128)(2,1)}, u32[]{:S(2)}, u32[]{:S(2)}) async-start(bf16[16,2,128,512]{3,2,1,0:T(8,128)(2,1)} %broadcast_select_fusion), calls=%async_computation.1 | async-start | bytes 8388608 | tf_op jit(solution)/shard_map/all_to_all | solution.py:123
  24.1 0.0 copy-start.2
  24.1 0.0 copy-start.3
  24.2 0.0 copy-start.4
  24.2 8.6 %copy.50 = bf16[32,384,256]{1,2,0:T(8,128)(2,1)} copy(bf16[32,384,256]{2,1,0:T(8,128)(2,1)} %param.10) | data formatting | bytes 12582912 | tf_op args[2]
  32.8 0.0 copy-done.2
  32.8 0.0 copy-done.3
  32.9 0.0 copy-done.4
  32.9 0.1 iota_compare_fusion
  33.0 2.6 %select_reduce_fusion = (f32[32,8]{1,0:T(8,128)S(1)}, f32[32,8,384]{2,1,0:T(8,128)S(1)}) fusion(pred[32,384]{1,0:T(8,128)(4,1)S(1)} %get-tuple-element.22, bf16[32,8,128]{2,1,0:T(8,128)(2,1)S(1)} %bitcast.121, bf16[32,384,1,2,128]{1,4,3,0,2:T(8,128)(2,1)} %bitcast.111), kind=kOutput, calls=%fused_computation.35 | convolution fusion | flops 25460480 | bytes 3617792 | tf_op jit(solution)/shard_map/nkgd,nlkd->nkgl/dot_general | solution.py:18
  35.6 0.2 convert_reduce_fusion
  35.9 0.1 fusion.17
  36.1 3.1 %fusion.8 = bf16[32,8,128]{2,1,0:T(8,128)(2,1)S(1)} fusion(bf16[32,384,1,2,128]{1,4,3,0,2:T(8,128)(2,1)} %bitcast.112, f32[32,8]{1,0:T(8,128)S(1)} %get-tuple-element.2, f32[32,8]{1,0:T(8,128)S(1)} %get-tuple-element.3, f32[32,128]{1,0:T(8,128)S(1)} %bitcast.127, f32[32,8]{1,0:T(8,128)S(1)} %get-tuple-element.4, f32[32,8,384]{2,1,0:T(8,128)S(1)} %get-tuple-element.32, ...), kind=kOutput, calls=%fused_computation.25 | convolution fusion | flops 25722880 | bytes 3637248 | tf_op jit(solution)/shard_map/nkgl,nlkd->nkgd/dot_general | solution.py:27
  39.2 0.1 reshape_reshape_reshape.3
  39.3 46.3 %all-to-all-done.1 = bf16[16,2,128,512]{3,2,1,0:T(8,128)(2,1)} async-done(((bf16[16,2,128,512]{3,2,1,0:T(8,128)(2,1)}), bf16[16,2,128,512]{3,2,1,0:T(8,128)(2,1)}, u32[]{:S(2)}, u32[]{:S(2)}) %all-to-all-start.1) | async-done | bytes 4194336 | tf_op jit(solution)/shard_map/all_to_all | solution.py:123
  85.6 3.1 %constant_dynamic-slice_fusion = bf16[32,128,256]{2,1,0:T(8,128)(2,1)} fusion(bf16[32,128,512]{2,1,0:T(8,128)(2,1)} %bitcast.13, s32[]{:T(128)S(6)} %select_n.167), kind=kLoop, calls=%fused_computation.92 | loop fusion | bytes 4194308 | tf_op jit(solution)/shard_map/dynamic_slice | solution.py:148
  88.7 1.5 collective-permute-start
  90.2 0.2 fusion.9
  90.5 0.2 convolution_convert_fusion.1
  90.7 0.1 select_reduce_fusion.3
  90.8 0.8 gather_fusion.4
  91.6 0.1 fusion.16
  91.7 0.1 iota_compare_fusion.4
  91.8 0.1 iota_compare_fusion.2
  91.9 0.1 fusion.18
  92.0 44.9 %collective-permute-done = bf16[32,128,256]{2,1,0:T(8,128)(2,1)} collective-permute-done((bf16[32,128,256]{2,1,0:T(8,128)(2,1)}, bf16[32,128,256]{2,1,0:T(8,128)(2,1)}, u32[]{:S(2)}, u32[]{:S(2)}) %collective-permute-start) | collective-permute-done | bytes 2097184 | tf_op jit(solution)/shard_map/ppermute | solution.py:14
  136.9 3.4 %broadcast_select_fusion.2 = (bf16[32,128,256]{2,1,0:T(8,128)(2,1)S(1)}, bf16[32,128,256]{2,1,0:T(8,128)(2,1)S(1)}) fusion(bf16[32,128,256]{2,1,0:T(8,128)(2,1)} %collective-permute-done, pred[]{:T(512)S(6)} %eq.100, bf16[32,128,512]{2,1,0:T(8,128)(2,1)} %bitcast.13, s32[]{:T(128)S(6)} %select_n.166), kind=kLoop, calls=%fused_computation.14 | loop fusion | flops 2097152 | bytes 8388613 | tf_op jit(solution)/shard_map/jit(_where)/select_n | solution.py:152
  140.3 2.5 pad_maximum_fusion
  142.7 6.4 %copy.45 = bf16[32,256,256]{1,2,0:T(8,128)(2,1)} copy(bf16[32,256,256]{2,1,0:T(8,128)(2,1)} %pad_maximum_fusion) | data formatting | bytes 8388608 | tf_op jit(solution)/shard_map/concatenate | solution.py:150
  149.2 1.7 select_reduce_fusion.2
  150.8 1.7 select_reduce_fusion.1
  152.5 0.3 convert_reduce_fusion.1
  152.8 1.9 convolution_multiply_fusion
  154.7 2.0 fusion.5
  156.7 4.9 %gather_fusion.5 = bf16[32,256,256]{2,1,0:T(8,128)(2,1)} fusion(bf16[32,256,256]{2,1,0:T(8,128)(2,1)} %pad_maximum_fusion, s32[1024]{0:T(1024)S(1)} %pad_clamp_fusion), kind=kCustom, calls=%fused_computation.5 | custom fusion | bytes 8388736 | tf_op jit(solution)/shard_map/gather | solution.py:179
  161.6 0.6 gather_fusion.3
  162.3 8.8 %fusion.11 = f32[32,8192]{1,0:T(8,128)S(1)} fusion(bf16[1024,8192]{1,0:T(8,128)(2,1)} %param.15, bf16[32,1024]{1,0:T(8,128)(2,1)S(1)} %gather_fusion.3, bf16[4,8,8,128]{3,2,1,0:T(8,128)(2,1)S(1)} %bitcast.124, pred[32]{0:T(512)(128)(4,1)S(1)} %fusion.16), kind=kOutput, calls=%fused_computation.45 | convolution fusion | flops 536903680 | bytes 17956896 | tf_op jit(solution)/shard_map/dot_general | solution.py:176
  171.0 79.8 %all-reduce.3 = bf16[32,8192]{1,0:T(8,128)(2,1)} all-reduce(f32[32,8192]{1,0:T(8,128)S(1)} %fusion.11), channel_id=1, replica_groups=mesh['rep'=16,'tp'=8] {'tp'}, use_global_device_ids=true, to_apply=%region_11.12 | all-reduce | flops 262144 | bytes 1572864 | tf_op jit(solution)/shard_map/psum | solution.py:177
  250.9 0.0 copy-start.1
  250.9 8.1 %select_select_fusion = bf16[32,384,256]{2,1,0:T(8,128)(2,1)} fusion(bf16[32,384,256]{2,1,0:T(8,128)(2,1)} %param.10, bf16[32,256,256]{2,1,0:T(8,128)(2,1)} %gather_fusion.5, pred[32]{0:T(512)(128)(4,1)S(1)} %fusion.16, pred[32,384]{1,0:T(8,128)(4,1)S(1)} %get-tuple-element.21, pred[32,384]{1,0:T(8,128)(4,1)S(1)} %get-tuple-element.18, ...), kind=kLoop, calls=%fused_computation.6 | loop fusion | flops 12582912 | bytes 16830496 | tf_op jit(solution)/shard_map/jit(_where)/select_n | solution.py:188
  258.9 0.0 copy-done.1
  (20 shorter events, 0.2 us)
Async XLA Ops:
  0.6 10.4 %copy-start = (bf16[16,1,128,512]{3,2,1,0:T(8,128)(2,1)S(1)}, bf16[16,1,128,512]{3,2,1,0:T(8,128)(2,1)}, u32[]{:S(2)}) copy-start(bf16[16,1,128,512]{3,2,1,0:T(8,128)(2,1)} %param.12) | copy-start | bytes 6291460
  5.4 13.0 %all-to-all-start = ((s32[16,2,2]{1,2,0:T(2,128)}), s32[16,2,2]{1,2,0:T(2,128)S(1)}, u32[]{:S(2)}, u32[]{:S(2)}) async-start(s32[16,2,2]{1,2,0:T(2,128)} %copy.42), calls=%async_computation | async-start | bytes 32768 | tf_op jit(solution)/shard_map/all_to_all | solution.py:124
  18.4 67.2 %all-to-all-start.1 = ((bf16[16,2,128,512]{3,2,1,0:T(8,128)(2,1)}), bf16[16,2,128,512]{3,2,1,0:T(8,128)(2,1)}, u32[]{:S(2)}, u32[]{:S(2)}) async-start(bf16[16,2,128,512]{3,2,1,0:T(8,128)(2,1)} %broadcast_select_fusion), calls=%async_computation.1 | async-start | bytes 8388608 | tf_op jit(solution)/shard_map/all_to_all | solution.py:123
  24.1 8.7 %copy-start.2 = (bf16[32,1024]{1,0:T(8,128)(2,1)S(1)}, bf16[32,1024]{1,0:T(8,128)(2,1)}, u32[]{:S(2)}) copy-start(bf16[32,1024]{1,0:T(8,128)(2,1)} %param.8) | copy-start | bytes 196612
  24.1 8.7 %copy-start.3 = (bf16[32,256]{1,0:T(8,128)(2,1)S(1)}, bf16[32,256]{1,0:T(8,128)(2,1)}, u32[]{:S(2)}) copy-start(bf16[32,256]{1,0:T(8,128)(2,1)} %param.9) | copy-start | bytes 49156
  24.2 8.7 %copy-start.4 = (s32[1,32]{1,0:T(1,128)S(1)}, s32[1,32]{1,0:T(1,128)}, u32[]{:S(2)}) copy-start(s32[1,32]{1,0:T(1,128)} %param.11) | copy-start | bytes 388
  88.7 48.1 %collective-permute-start = (bf16[32,128,256]{2,1,0:T(8,128)(2,1)}, bf16[32,128,256]{2,1,0:T(8,128)(2,1)}, u32[]{:S(2)}, u32[]{:S(2)}) collective-permute-start(bf16[32,128,256]{2,1,0:T(8,128)(2,1)} %constant_dynamic-slice_fusion), channel_id=1, source_target_pairs={{0,1},{1,0},{2,3},{3,2},{4,5},{5,4},{6,7},{7,6},{8,9},{9,8},{10,11... | collective-permute-start | bytes 6291464 | tf_op jit(solution)/shard_map/ppermute | solution.py:14
  250.9 8.1 %copy-start.1 = (bf16[16,1,128,512]{3,2,1,0:T(8,128)(2,1)S(1)}, bf16[16,1,128,512]{3,2,1,0:T(8,128)(2,1)}, u32[]{:S(2)}) copy-start(bf16[16,1,128,512]{3,2,1,0:T(8,128)(2,1)} %param.12) | copy-start | bytes 6291460
where the time goes:
time: 260 us; the launch traced here: 259 us
  waiting for transfers between devices  91.2 us (35%)
  blocking collectives  79.8 us (31%)
  local copies, waits for them, and re-layouts  31.3 us (12%)
  matrix products  22.4 us (9%)
  other arithmetic  20.5 us (8%)
  starting transfers between devices  12.8 us (5%)
    psum x1, blocking collectives, body(): attended = lax.psum(head_terms, 'tp').astype(jnp.bfloat16)  79.8 us
    all_to_all x1, waiting for transfers between devices, body(): lax.all_to_all(packed, 'rep', split_axis=0, concat_axis=0, tiled=True)  46.3 us
    ppermute x1, waiting for transfers between devices, from_partner(): lax.ppermute(array, axis, [(i, i ^ 1 << bit) for i in range(lax.axis_size...  44.9 us
    dot_general x1, matrix products, body(): jnp.dot(attention_rows, out_weight, preferred_element_type=jnp.float32)  8.77 us
    unnamed x15, local copies, waits for them, and re-layouts  8.72 us
    select_n x1, other arithmetic, body(): updated = jnp.where(replaced[:, None, None], installed, resident_kept)  8.07 us
    dot_general x3, matrix products, partial_softmax(): jnp.einsum('nkgl,nlkd->nkgd', weights, value_rows, preferred_element_type...  6.98 us
    concatenate x1, local copies, waits for them, and re-layouts, body(): jnp.concatenate([jnp.where(parity == 0, own_piece, partner_half), jnp.whe...  6.41 us
  transfers between devices with their start and end apart: 3, of which 2 were waited for; matrix products, arithmetic and copies ran while one was open for 9% of the time, Pallas kernels for 0%

commit v1 on v0

--- a/solution.py
+++ b/solution.py
@@ -1,17 +1,222 @@
+import functools
+
 import jax
 import jax.numpy as jnp
 from jax import lax
+from jax.experimental import pallas as pl
+from jax.experimental.pallas import tpu as pltpu
 from jax.sharding import PartitionSpec as P
 
 HEAD = 128
 CAP = 2
-
-
 NEG_FILL = -1e30
-
-
-def from_partner(array, axis, bit):
-    return lax.ppermute(array, axis, [(i, i ^ 1 << bit) for i in range(lax.axis_size(axis))])
+MESH = pl.DeviceIdType.MESH
+
+REP_STEPS = [
+    (y, z, c)
+    for z in (1, 3, 2, 0)
+    for y in (1, 0)
+    for c in (0, 1)
+    if (y, z, c) != (0, 0, 0)
+]
+TP_STEPS = [(h, x) for x in (2, 1, 3, 0) for h in (1, 0) if (h, x) != (0, 0)]
+
+
+def rep_at(rep, step, sign):
+    y, z, c = rep // 8, (rep // 2) % 4, rep % 2
+    dy, dz, dc = step
+    return ((y + dy) % 2) * 8 + ((z + sign * dz + 4) % 4) * 2 + (c + dc) % 2
+
+
+def tp_at(tp, step, sign):
+    h, x = tp // 4, tp % 4
+    dh, dx = step
+    return ((h + dh) % 2) * 4 + (x + sign * dx + 4) % 4
+
+
+def handoff_kernel(
+    hand_s, hand_ref, len_ref, caches, arrived, hand_all, len_all,
+    own, other, packed, own_sem, pair_send, pair_recv, send, recv, stay, mh_send, mh_recv, ml_send, ml_recv,
+):
+    rep, tp = lax.axis_index("rep"), lax.axis_index("tp")
+    parity = tp % 2
+    partner = tp + 1 - 2 * parity
+    width = own.shape[2]
+    half = own.shape[1]
+    count = own.shape[0]
+    mine = pl.ds(pl.multiple_of(parity * width, width), width)
+    theirs = pl.ds(pl.multiple_of((1 - parity) * width, width), width)
+    load = pltpu.make_async_copy(caches.at[:, 0, :, mine], own, own_sem)
+    load.start()
+
+    barrier = pltpu.get_barrier_semaphore()
+    for step in REP_STEPS:
+        pl.semaphore_signal(barrier, inc=1, device_id=(rep_at(rep, step, -1), tp), device_id_type=MESH)
+    pl.semaphore_signal(barrier, inc=1, device_id=(rep, partner), device_id_type=MESH)
+    pl.semaphore_wait(barrier, len(REP_STEPS) + 1)
+
+    pair = pltpu.make_async_remote_copy(
+        src_ref=caches.at[:, 0, :, theirs], dst_ref=other, send_sem=pair_send, recv_sem=pair_recv,
+        device_id=(rep, partner), device_id_type=MESH,
+    )
+    pair.start()
+    copies = []
+    for k, step in enumerate(REP_STEPS):
+        to = (rep_at(rep, step, 1), tp)
+        for src, dst, s, r in (
+            (hand_ref.at[0], hand_all.at[rep], mh_send, mh_recv),
+            (len_ref, len_all.at[rep], ml_send, ml_recv),
+        ):
+            copy = pltpu.make_async_remote_copy(
+                src_ref=src, dst_ref=dst, send_sem=s.at[k], recv_sem=r.at[k], device_id=to, device_id_type=MESH
+            )
+            copy.start()
+            copies.append(copy)
+    hand_all[rep] = hand_ref[0]
+    len_all[rep] = len_ref[...]
+
+    targets = [hand_s[0, i, 0] for i in range(count)]
+
+    def sources(group):
+        seen, first, second = jnp.int32(0), jnp.int32(0), jnp.int32(0)
+        for i in range(count):
+            hit = targets[i] == group
+            first = jnp.where(hit & (seen == 0), i, first)
+            second = jnp.where(hit & (seen == 1), i, second)
+            seen = seen + hit.astype(jnp.int32)
+        return first, second
+
+    picks = [sources(rep_at(rep, step, 1)) for step in REP_STEPS]
+    picks.append(sources(rep))
+    slots = pl.ds(rep * CAP, CAP)
+    for phase, held in ((0, own), (1, other)):
+        if phase == 0:
+            load.wait()
+        else:
+            pair.wait()
+        part = parity if phase == 0 else 1 - parity
+        tokens = pl.ds(pl.multiple_of(part * half, half), half)
+        for k, step in enumerate(REP_STEPS):
+            first, second = picks[k]
+            packed[phase, k, 0] = held[first]
+            packed[phase, k, 1] = held[second]
+            copy = pltpu.make_async_remote_copy(
+                src_ref=packed.at[phase, k], dst_ref=arrived.at[slots, tokens, :],
+                send_sem=send.at[phase, k], recv_sem=recv.at[phase, k],
+                device_id=(rep_at(rep, step, 1), tp), device_id_type=MESH,
+            )
+            copy.start()
+            copies.append(copy)
+        k = len(REP_STEPS)
+        packed[phase, k, 0] = held[picks[k][0]]
+        packed[phase, k, 1] = held[picks[k][1]]
+        copy = pltpu.make_async_copy(packed.at[phase, k], arrived.at[slots, tokens, :], stay.at[phase])
+        copy.start()
+        copies.append(copy)
+    for copy in copies:
+        copy.wait()
+
+
+def hand_off(handoff, new_lengths, new_caches):
+    count, _, half, wide = new_caches.shape
+    width = wide // 2
+    groups = lax.axis_size("rep")
+    peers = len(REP_STEPS)
+    dma = pltpu.SemaphoreType.DMA
+    vmem = pl.BlockSpec(memory_space=pltpu.VMEM)
+    return pl.pallas_call(
+        handoff_kernel,
+        out_shape=(
+            jax.ShapeDtypeStruct((groups * CAP, 2 * half, width), new_caches.dtype),
+            jax.ShapeDtypeStruct((groups,) + handoff.shape[1:], handoff.dtype),
+            jax.ShapeDtypeStruct((groups,) + new_lengths.shape, new_lengths.dtype),
+        ),
+        in_specs=[pl.BlockSpec(memory_space=pltpu.SMEM), vmem, vmem, pl.BlockSpec(memory_space=pl.ANY)],
+        out_specs=(pl.BlockSpec(memory_space=pl.ANY), vmem, vmem),
+        scratch_shapes=[
+            pltpu.VMEM((count, half, width), new_caches.dtype),
+            pltpu.VMEM((count, half, width), new_caches.dtype),
+            pltpu.VMEM((2, groups, CAP, half, width), new_caches.dtype),
+            dma, dma, dma, dma((2, peers)), dma((2, peers)), dma((2,)),
+            dma((peers,)), dma((peers,)), dma((peers,)), dma((peers,)),
+        ],
+        compiler_params=pltpu.CompilerParams(
+            collective_id=0, has_side_effects=True, vmem_limit_bytes=24 * 2**20
+        ),
+        name="hand_off",
+    )(handoff, handoff, new_lengths, new_caches)
+
+
+def project_kernel(rows, weight, out, held, staged, parts, load, rs_send, rs_recv, ag_send, ag_recv):
+    rep, tp = lax.axis_index("rep"), lax.axis_index("tp")
+    width = staged.shape[2]
+    steps = TP_STEPS + [(0, 0)]
+    last = len(TP_STEPS)
+    loads = []
+    for k, step in enumerate(steps):
+        at = pl.multiple_of(tp_at(tp, step, 1) * width, width)
+        copy = pltpu.make_async_copy(weight.at[:, pl.ds(at, width)], held.at[k], load.at[k])
+        copy.start()
+        loads.append(copy)
+    barrier = pltpu.get_barrier_semaphore()
+    for step in TP_STEPS:
+        pl.semaphore_signal(barrier, inc=1, device_id=(rep, tp_at(tp, step, -1)), device_id_type=MESH)
+    pl.semaphore_wait(barrier, len(TP_STEPS))
+    scatter = []
+    for k, step in enumerate(TP_STEPS):
+        loads[k].wait()
+        staged[k] = jnp.dot(rows[...], held[k], preferred_element_type=jnp.float32).astype(staged.dtype)
+        copy = pltpu.make_async_remote_copy(
+            src_ref=staged.at[k], dst_ref=parts.at[k], send_sem=rs_send.at[k], recv_sem=rs_recv.at[k],
+            device_id=(rep, tp_at(tp, step, 1)), device_id_type=MESH,
+        )
+        copy.start()
+        scatter.append(copy)
+    loads[last].wait()
+    total = jnp.dot(rows[...], held[last], preferred_element_type=jnp.float32)
+    for k in range(last):
+        scatter[k].wait_recv()
+        total = total + parts[k].astype(jnp.float32)
+    columns = pl.ds(pl.multiple_of(tp * width, width), width)
+    out[:, columns] = total.astype(out.dtype)
+    gather = []
+    for k, step in enumerate(TP_STEPS):
+        copy = pltpu.make_async_remote_copy(
+            src_ref=out.at[:, columns], dst_ref=out.at[:, columns], send_sem=ag_send.at[k], recv_sem=ag_recv.at[k],
+            device_id=(rep, tp_at(tp, step, 1)), device_id_type=MESH,
+        )
+        copy.start()
+        gather.append(copy)
+    for copy in scatter:
+        copy.wait_send()
+    for copy in gather:
+        copy.wait()
+
+
+def project(rows, weight):
+    count, depth = rows.shape
+    columns = weight.shape[1]
+    shares = lax.axis_size("tp")
+    width = columns // shares
+    peers = len(TP_STEPS)
+    dma = pltpu.SemaphoreType.DMA
+    vmem = pl.BlockSpec(memory_space=pltpu.VMEM)
+    return pl.pallas_call(
+        project_kernel,
+        out_shape=jax.ShapeDtypeStruct((count, columns), rows.dtype),
+        in_specs=[vmem, pl.BlockSpec(memory_space=pl.ANY)],
+        out_specs=vmem,
+        scratch_shapes=[
+            pltpu.VMEM((shares, depth, width), weight.dtype),
+            pltpu.VMEM((peers, count, width), rows.dtype),
+            pltpu.VMEM((peers, count, width), rows.dtype),
+            dma((shares,)), dma((peers,)), dma((peers,)), dma((peers,)), dma((peers,)),
+        ],
+        compiler_params=pltpu.CompilerParams(
+            collective_id=1, has_side_effects=True, vmem_limit_bytes=32 * 2**20
+        ),
+        name="project",
+    )(rows, weight)
 
 
 def partial_softmax(query_rows, key_rows, value_rows, valid_mask):
@@ -81,7 +286,6 @@
     half_len = new_caches.shape[2]
     group_count = lax.axis_size("rep")
     entries = group_count * CAP
-    parity = lax.axis_index("tp") % 2
     query_rows = queries.reshape(row_count, kv_here, per_kv, HEAD)
     own_view = new_token_kv.reshape(row_count, kv_here, 2, HEAD)
     own_score = jnp.einsum(
@@ -98,73 +302,30 @@
         positions[None, :] < lengths_here[:, None],
     )
     resident_out = combine_partials([resident_part], own_score, own_value)
-    dest_group = handoff[0, :, 0]
-    dest_row = handoff[0, :, 1]
-    request_lengths = new_lengths[0]
-    request_count = dest_group.shape[0]
-    request_ids = jnp.arange(request_count, dtype=jnp.int32)
-    earlier = (dest_group[:, None] == dest_group[None, :]) & (
-        request_ids[None, :] < request_ids[:, None]
-    )
-    slot_index = dest_group * CAP + jnp.sum(earlier.astype(jnp.int32), axis=1)
-    matches = slot_index[None, :] == jnp.arange(entries, dtype=jnp.int32)[:, None]
-    filled = jnp.any(matches, axis=1)
-    source = jnp.sum(jnp.where(matches, request_ids[None, :], 0), axis=1)
-    metadata = jnp.stack(
-        [jnp.where(filled, dest_row[source], -1), jnp.where(filled, request_lengths[source], 0)],
-        axis=1,
-    )
-    metadata = metadata.reshape(group_count, CAP, 2)
-    prefill_pieces = new_caches[:, 0]
-    packed = jnp.where(
-        filled[:, None, None], prefill_pieces[source], jnp.zeros((), prefill_pieces.dtype)
-    )
-    packed = packed.reshape(group_count, CAP, prefill_pieces.shape[1], prefill_pieces.shape[2])
-    buffer = lax.all_to_all(packed, "rep", split_axis=0, concat_axis=0, tiled=True)
-    incoming = lax.all_to_all(metadata, "rep", split_axis=0, concat_axis=0, tiled=True)
-    sources = buffer.shape[0]
-    item_count = buffer.shape[1]
-    entry_count = sources * item_count
-    flattened = buffer.reshape(entry_count, buffer.shape[2], buffer.shape[3])
-    incoming = incoming.reshape(entry_count, 2)
-    rows_of = incoming[:, 0]
-    lengths_of = incoming[:, 1]
-    selector = (rows_of[:, None] == jnp.arange(row_count, dtype=jnp.int32)[None, :]).astype(
-        jnp.bfloat16
-    )
+    full_heads, hand_all, len_all = hand_off(handoff, new_lengths, new_caches)
+    len_all = len_all[:, 0]
+    to_me = hand_all[:, :, 0] == lax.axis_index("rep")
+    rank = jnp.cumsum(to_me.astype(jnp.int32), axis=1) - 1
+    pick = to_me[:, None, :] & (rank[:, None, :] == jnp.arange(CAP, dtype=jnp.int32)[None, :, None])
+    filled = jnp.any(pick, axis=2)
+    rows_of = jnp.where(filled, jnp.sum(jnp.where(pick, hand_all[:, None, :, 1], 0), axis=2), -1).reshape(entries)
+    lengths_of = jnp.sum(jnp.where(pick, len_all[:, None, :], 0), axis=2).reshape(entries)
+    matches_rows = rows_of[:, None] == jnp.arange(row_count, dtype=jnp.int32)[None, :]
+    selector = matches_rows.astype(jnp.bfloat16)
     entry_queries = jnp.dot(selector, queries, preferred_element_type=jnp.float32).astype(
         jnp.bfloat16
     )
-    entry_queries = entry_queries.reshape(entry_count, kv_here, per_kv, HEAD)
+    entry_queries = entry_queries.reshape(entries, kv_here, per_kv, HEAD)
     entry_own = jnp.dot(selector, new_token_kv, preferred_element_type=jnp.float32).astype(
         jnp.bfloat16
     )
-    entry_own = entry_own.reshape(entry_count, kv_here, 2, HEAD)
+    entry_own = entry_own.reshape(entries, kv_here, 2, HEAD)
     entry_score = jnp.einsum(
         "nkgd,nkd->nkg", entry_queries, entry_own[:, :, 0, :], preferred_element_type=jnp.float32
     ) * HEAD ** (-0.5)
     entry_value = entry_own[:, :, 1, :].astype(jnp.float32)
-    own_piece = lax.dynamic_slice_in_dim(flattened, parity * piece_width, piece_width, 2)
-    theirs = lax.dynamic_slice_in_dim(flattened, (1 - parity) * piece_width, piece_width, 2)
-    partner_half = from_partner(theirs, "tp", 0)
-    full_heads = jnp.concatenate(
-        [
-            jnp.where(parity == 0, own_piece, partner_half),
-            jnp.where(parity == 0, partner_half, own_piece),
-        ],
-        axis=1,
-    )
     pieces_list = take_halves(full_heads, entry_queries, lengths_of, half_len)
-    entry_out = combine_partials(pieces_list, entry_score, entry_value)
-    entry_out, full_heads, incoming = (
-        entry_out.reshape(sources, item_count, -1),
-        full_heads.reshape(sources, item_count, 2 * half_len, piece_width),
-        incoming.reshape(sources, item_count, 2),
-    )
-    entry_out = entry_out.reshape(entries, -1)
-    full_heads = full_heads.reshape(entries, 2 * half_len, piece_width)
-    incoming = incoming.reshape(entries, 2)
-    matches_rows = incoming[:, 0][:, None] == jnp.arange(row_count, dtype=jnp.int32)[None, :]
+    entry_out = combine_partials(pieces_list, entry_score, entry_value).reshape(entries, -1)
     replaced = jnp.any(matches_rows, axis=0)
     entry_index = jnp.sum(
         jnp.where(matches_rows, jnp.arange(entries, dtype=jnp.int32)[:, None], 0), axis=0
@@ -173,9 +334,8 @@
     attention_rows = jnp.where(
         replaced[:, None], arrived_out, resident_out.reshape(row_count, -1)
     ).astype(jnp.bfloat16)
-    head_terms = jnp.dot(attention_rows, out_weight, preferred_element_type=jnp.float32)
-    attended = lax.psum(head_terms, "tp").astype(jnp.bfloat16)
-    arrived_len = jnp.where(replaced, incoming[entry_index, 1], 0)
+    attended = project(attention_rows, out_weight)
+    arrived_len = jnp.where(replaced, lengths_of[entry_index], 0)
     padded = jnp.pad(full_heads[entry_index], ((0, 0), (0, cache_len - 2 * half_len), (0, 0)))
     slot_ids = positions[None, :, None]
     own_flat = new_token_kv[:, None, :]

time: 260 us -> 152 us (0.58)
  the two profiles are of different devices: /device:TPU:96 before, /device:TPU:0 now
where the time goes in v1:
time: 152 us; the launch traced here: 151 us
  Pallas kernels  82.7 us (54%)
  local copies, waits for them, and re-layouts  44.5 us (29%)
  matrix products  13.6 us (9%)
  other arithmetic  9.82 us (6%)
    pallas_call x1, Pallas kernels, hand_off(): pl.pallas_call(handoff_kernel, out_shape=(jax.ShapeDtypeStruct((groups *...  56.3 us
    pallas_call x1, Pallas kernels, project(): pl.pallas_call(project_kernel, out_shape=jax.ShapeDtypeStruct((count, col...  26.4 us
    unnamed x21, local copies, waits for them, and re-layouts  20.2 us
    slice x1, local copies, waits for them, and re-layouts, take_halves(): cache_view[:, :half_len, :, 1, :]  10.3 us
    select_n x1, other arithmetic, body(): updated = jnp.where(replaced[:, None, None], installed, resident_kept)  7.93 us
    dot_general x3, matrix products, partial_softmax(): jnp.einsum('nkgl,nlkd->nkgd', weights, value_rows, preferred_element_type...  7.22 us
    reshape x1, local copies, waits for them, and re-layouts, take_halves(): cache_view = full_heads.reshape(entry_count, 2 * half_len, -1, 2, HEAD)  6.88 us
    dot_general x3, matrix products, partial_softmax(): jnp.einsum('nkgd,nlkd->nkgl', query_rows, key_rows, preferred_element_typ...  5.68 us

profile of v1, /device:TPU:0, one launch (start us, length us, event | category | flops | bytes accessed | tf_op | source)
XLA Modules:
  0.0 151.4 jit_solution(4523916740809806151)
XLA Ops:
  0.6 0.8 copy.37.hand_s.hand_ref
  1.4 0.0 copy-start.2
  1.4 1.6 %copy-done.2 = bf16[16,1,128,512]{3,2,1,0:T(8,128)(2,1)S(1)} copy-done((bf16[16,1,128,512]{3,2,1,0:T(8,128)(2,1)S(1)}, bf16[16,1,128,512]{3,2,1,0:T(8,128)(2,1)}, u32[]{:S(2)}) %copy-start.2) | copy-done | bytes 2097176
  3.0 0.0 copy-start.3
  3.0 0.7 copy-done.3
  3.6 56.3 %hand_off.1 = (bf16[32,256,256]{2,1,0:T(8,128)(2,1)S(1)}, s32[16,16,2]{2,1,0:T(8,128)S(1)}, s32[16,1,16]{2,1,0:T(1,128)S(1)}) custom-call(s32[1,16,2]{2,1,0:T(8,128)S(1)} %copy.37.hand_s.hand_ref, s32[1,16,2]{2,1,0:T(8,128)S(1)} %copy.37.hand_s.hand_ref, s32[1,16]{1,0:T(1,128)S(1)} %copy-done.3, bf16[16,1,128,512]{3,2,1,0:T(8,128)(2,1)S(1)} %copy-done.2), custom_call_target="tpu_custom_call" | custom-call | tf_op jit(solution)/shard_map/hand_off/pallas_call | solution.py:127
  60.0 0.0 copy-start.1
  60.0 1.9 %copy-done.1 = bf16[32,256,256]{2,1,0:T(8,128)(2,1)} copy-done((bf16[32,256,256]{2,1,0:T(8,128)(2,1)}, bf16[32,256,256]{2,1,0:T(8,128)(2,1)S(1)}, u32[]{:S(2)}) %copy-start.1) | copy-done | bytes 4194328
  61.9 6.9 %reshape.421 = bf16[32,256,1,2,128]{4,3,1,0,2:T(2,128)(2,1)} reshape(bf16[32,256,256]{2,1,0:T(8,128)(2,1)} %copy-done.1) | data formatting | bytes 8388608 | tf_op jit(solution)/shard_map/reshape | solution.py:254
  68.8 0.0 copy-start.4
  68.8 0.0 copy-start.5
  68.8 10.3 %fusion.25 = (bf16[32,128,1,1,128]{4,3,1,0,2:T(2,128)(2,1)}, bf16[32,128,1,1,128]{4,3,1,0,2:T(2,128)(2,1)}, bf16[32,128,1,1,128]{4,3,1,0,2:T(2,128)(2,1)S(1)}, bf16[32,128,1,1,128]{4,3,1,0,2:T(2,128)(2,1)}) fusion(bf16[32,256,1,2,128]{4,3,1,0,2:T(2,128)(2,1)} %reshape.421), kind=kLoop, calls=%fused_computation.81 | loop fusion | bytes 8388608 | tf_op jit(solution)/shard_map/slice | solution.py:259
  79.1 0.4 fusion.11
  79.5 0.2 reduce_window_sum.11
  79.6 0.4 slice_reduce_fusion
  80.1 0.2 select_reduce_fusion.4
  80.2 0.1 copy.41
  80.3 0.1 lt.80
  80.4 0.1 iota_compare_fusion.4
  80.5 0.1 fusion.19
  80.6 0.1 copy.39
  80.7 0.1 select_n.103
  80.8 0.0 copy-done.4
  80.8 0.2 fusion.9
  81.0 2.3 %select_reduce_fusion.1 = (f32[32,8]{1,0:T(8,128)S(1)}, f32[32,8,128]{2,1,0:T(8,128)S(1)}) fusion(pred[32,128]{1,0:T(8,128)(4,1)S(1)} %get-tuple-element.28, bf16[32,8,128]{2,1,0:T(8,128)(2,1)S(1)} %bitcast.80, bf16[32,128,1,1,128]{4,3,1,0,2:T(2,128)(2,1)} %get-tuple-element.18), kind=kOutput, calls=%fused_computation.36 | convolution fusion | flops 8486656 | bytes 1250304 | tf_op jit(solution)/shard_map/nkgd,nlkd->nkgl/dot_general | solution.py:223
  83.3 0.7 select_reduce_fusion.2
  84.1 0.3 convert_reduce_fusion.1
  84.4 0.0 copy-done.5
  84.4 0.2 convolution_convert_fusion.1
  84.6 0.1 fusion.16
  84.8 2.0 %convolution_multiply_fusion = f32[32,8,128]{2,1,0:T(8,128)S(1)} fusion(bf16[32,128,1,1,128]{4,3,1,0,2:T(2,128)(2,1)} %get-tuple-element.20, f32[32,8]{1,0:T(8,128)S(1)} %get-tuple-element.16, f32[32,8,128]{2,1,0:T(8,128)S(1)} %get-tuple-element.30, f32[32,8]{1,0:T(8,128)S(1)} %get-tuple-element.29, pred[32,128]{1,0:T(8,128)(4,1)S(1)} %get-tuple-element.28), kind=kOutput, calls=%fused_computation.9 | convolution fusion | flops 8552448 | bytes 1316864 | tf_op jit(solution)/shard_map/nkgl,nlkd->nkgd/dot_general | solution.py:232
  86.8 2.1 %fusion.5 = bf16[32,8,128]{2,1,0:T(8,128)(2,1)S(1)} fusion(f32[32,8,128]{2,1,0:T(8,128)S(1)} %convolution_multiply_fusion, bf16[32,128,1,1,128]{4,3,1,0,2:T(2,128)(2,1)} %get-tuple-element.17, f32[32,8]{1,0:T(8,128)S(1)} %get-tuple-element.13, f32[32,8]{1,0:T(8,128)S(1)} %get-tuple-element.14, f32[32,128]{1,0:T(8,128)S(1)} %bitcast.90, ...), kind=kOutput, calls=%fused_computation.15 | convolution fusion | flops 8716288 | bytes 1400832 | tf_op jit(solution)/shard_map/nkgl,nlkd->nkgd/dot_general | solution.py:232
  88.9 0.1 select_reduce_fusion.3
  89.0 0.6 gather_fusion
  89.7 0.0 copy-start.6
  89.7 8.6 %copy.46 = bf16[32,384,256]{1,2,0:T(8,128)(2,1)} copy(bf16[32,384,256]{2,1,0:T(8,128)(2,1)} %param.10) | data formatting | bytes 12582912 | tf_op args[2]
  98.3 0.1 fusion.14
  98.4 0.7 gather_fusion.1
  99.1 0.0 copy-done.6
  99.1 0.1 iota_compare_fusion
  99.2 2.6 %select_reduce_fusion = (f32[32,8]{1,0:T(8,128)S(1)}, f32[32,8,384]{2,1,0:T(8,128)S(1)}) fusion(pred[32,384]{1,0:T(8,128)(4,1)S(1)} %get-tuple-element.26, bf16[32,8,128]{2,1,0:T(8,128)(2,1)S(1)} %bitcast.83, bf16[32,384,1,2,128]{1,4,3,0,2:T(8,128)(2,1)} %bitcast.77), kind=kOutput, calls=%fused_computation.28 | convolution fusion | flops 25460480 | bytes 3617792 | tf_op jit(solution)/shard_map/nkgd,nlkd->nkgl/dot_general | solution.py:223
  101.8 0.2 convert_reduce_fusion
  102.1 0.1 fusion.15
  102.3 3.1 %fusion.8 = bf16[32,8,128]{2,1,0:T(8,128)(2,1)S(1)} fusion(bf16[32,384,1,2,128]{1,4,3,0,2:T(8,128)(2,1)} %bitcast.78, f32[32,8]{1,0:T(8,128)S(1)} %get-tuple-element.10, f32[32,8]{1,0:T(8,128)S(1)} %get-tuple-element.11, f32[32,128]{1,0:T(8,128)S(1)} %bitcast.89, f32[32,8]{1,0:T(8,128)S(1)} %get-tuple-element.12, f32[32,8,384]{2,1,0:T(8,128)S(1)} %get-tuple-element.34, ...), kind=kOutput, calls=%fused_computation.18 | convolution fusion | flops 25722880 | bytes 3637248 | tf_op jit(solution)/shard_map/nkgl,nlkd->nkgd/dot_general | solution.py:232
  105.4 0.1 fusion.10.rows
  105.5 0.0 copy-start
  105.6 5.8 %copy-done = bf16[1024,8192]{1,0:T(8,128)(2,1)S(1)} copy-done((bf16[1024,8192]{1,0:T(8,128)(2,1)S(1)}, bf16[1024,8192]{1,0:T(8,128)(2,1)}, u32[]{:S(2)}) %copy-start) | copy-done | bytes 16777240
  111.3 26.4 %project.1 = bf16[32,8192]{1,0:T(8,128)(2,1)S(1)} custom-call(bf16[32,1024]{1,0:T(8,128)(2,1)S(1)} %fusion.10.rows, bf16[1024,8192]{1,0:T(8,128)(2,1)S(1)} %copy-done), custom_call_target="tpu_custom_call" | custom-call | tf_op jit(solution)/shard_map/project/pallas_call | solution.py:204
  137.7 5.0 %gather_fusion.2 = bf16[32,256,256]{2,1,0:T(8,128)(2,1)} fusion(bf16[32,256,256]{2,1,0:T(8,128)(2,1)} %copy-done.1, s32[1024]{0:T(1024)S(1)} %pad_clamp_fusion), kind=kCustom, calls=%fused_computation.2 | custom fusion | bytes 8388736 | tf_op jit(solution)/shard_map/gather | solution.py:339
  142.7 7.9 %select_select_fusion = bf16[32,384,256]{2,1,0:T(8,128)(2,1)} fusion(bf16[32,384,256]{2,1,0:T(8,128)(2,1)} %param.10, bf16[32,256,256]{2,1,0:T(8,128)(2,1)} %gather_fusion.2, pred[32]{0:T(512)(128)(4,1)S(1)} %fusion.14, pred[32,384]{1,0:T(8,128)(4,1)S(1)} %get-tuple-element.25, pred[32,384]{1,0:T(8,128)(4,1)S(1)} %get-tuple-element.37, ...), kind=kLoop, calls=%fused_computation.3 | loop fusion | flops 12582912 | bytes 16830496 | tf_op jit(solution)/shard_map/jit(_where)/select_n | solution.py:348
  150.6 0.8 copy.84
  (17 shorter events, 0.2 us)
Async XLA Ops:
  1.4 1.6 %copy-start.2 = (bf16[16,1,128,512]{3,2,1,0:T(8,128)(2,1)S(1)}, bf16[16,1,128,512]{3,2,1,0:T(8,128)(2,1)}, u32[]{:S(2)}) copy-start(bf16[16,1,128,512]{3,2,1,0:T(8,128)(2,1)} %caches.1) | copy-start | bytes 6291460
  3.0 0.7 copy-start.3
  60.0 1.9 %copy-start.1 = (bf16[32,256,256]{2,1,0:T(8,128)(2,1)}, bf16[32,256,256]{2,1,0:T(8,128)(2,1)S(1)}, u32[]{:S(2)}) copy-start(bf16[32,256,256]{2,1,0:T(8,128)(2,1)S(1)} %get-tuple-element.7) | copy-start | bytes 12582916
  68.8 12.0 %copy-start.4 = (bf16[32,1024]{1,0:T(8,128)(2,1)S(1)}, bf16[32,1024]{1,0:T(8,128)(2,1)}, u32[]{:S(2)}) copy-start(bf16[32,1024]{1,0:T(8,128)(2,1)} %param.8) | copy-start | bytes 196612
  68.8 15.6 %copy-start.5 = (bf16[32,256]{1,0:T(8,128)(2,1)S(1)}, bf16[32,256]{1,0:T(8,128)(2,1)}, u32[]{:S(2)}) copy-start(bf16[32,256]{1,0:T(8,128)(2,1)} %param.9) | copy-start | bytes 49156
  89.7 9.4 %copy-start.6 = (s32[1,32]{1,0:T(1,128)S(1)}, s32[1,32]{1,0:T(1,128)}, u32[]{:S(2)}) copy-start(s32[1,32]{1,0:T(1,128)} %param.11) | copy-start | bytes 388
  105.5 5.8 %copy-start = (bf16[1024,8192]{1,0:T(8,128)(2,1)S(1)}, bf16[1024,8192]{1,0:T(8,128)(2,1)}, u32[]{:S(2)}) copy-start(bf16[1024,8192]{1,0:T(8,128)(2,1)} %weight.1) | copy-start | bytes 50331652

commit v2 on v0

v2 whole, which is shorter than its diff:
```python
import functools

import jax
import jax.numpy as jnp
from jax import lax
from jax.experimental import pallas as pl
from jax.experimental.pallas import tpu as pltpu
from jax.sharding import PartitionSpec as P

HEAD = 128
CAP = 2
NEG_FILL = -1e30
SCALE = HEAD ** (-0.5)
MESH = pl.DeviceIdType.MESH
NO_ROW = 32
LEN_UNIT = 64
RES_PARTS = 4

REP_STEPS = [
    (y, z, c)
    for z in (1, 3, 2, 0)
    for y in (1, 0)
    for c in (0, 1)
    if (y, z, c) != (0, 0, 0)
]
TP_STEPS = [(h, x) for x in (2, 1, 3, 0) for h in (1, 0) if (h, x) != (0, 0)]


def rep_at(rep, step, sign):
    y, z, c = rep // 8, (rep // 2) % 4, rep % 2
    dy, dz, dc = step
    return ((y + dy) % 2) * 8 + ((z + sign * dz + 4) % 4) * 2 + (c + dc) % 2


def tp_at(tp, step, sign):
    h, x = tp // 4, tp % 4
    dh, dx = step
    return ((h + dh) % 2) * 4 + (x + sign * dx + 4) % 4


def iota(shape, dim):
    return lax.broadcasted_iota(jnp.int32, shape, dim)


def contract_last(a, b):
    return lax.dot_general(a, b, (((1,), (1,)), ((), ())), preferred_element_type=jnp.float32)


def contract_first(a, b):
    return lax.dot_general(a, b, (((0,), (0,)), ((), ())), preferred_element_type=jnp.float32)


def attend_pair(query_pair, kv_a, kv_b, limits):
    low = iota(query_pair.shape, 0) < 8
    zero = jnp.zeros_like(query_pair)
    blocks = jnp.concatenate([jnp.where(low, query_pair, zero), jnp.where(low, zero, query_pair)], axis=1)
    keys = jnp.concatenate([kv_a[:, :HEAD], kv_b[:, :HEAD]], axis=1)
    values = jnp.concatenate([kv_a[:, HEAD:], kv_b[:, HEAD:]], axis=1)
    scores = contract_last(blocks.astype(jnp.bfloat16), keys) * SCALE
    allowed = iota(scores.shape, 1) < limits
    peak = jnp.max(jnp.where(allowed, scores, NEG_FILL), axis=1, keepdims=True)
    weights = jnp.where(allowed, jnp.exp(jnp.where(allowed, scores, peak) - peak), 0.0).astype(jnp.bfloat16)
    total = jnp.sum(weights.astype(jnp.float32), axis=1, keepdims=True)
    both = jnp.dot(weights, values, preferred_element_type=jnp.float32)
    return peak, total, jnp.where(low, both[:, :HEAD], both[:, HEAD:])


def combine(peak, total, acc, own_score, own_value):
    top = jnp.maximum(peak, own_score)
    own_weight, factor = jnp.exp(own_score - top), jnp.exp(peak - top)
    return (own_weight * own_value + factor * acc) / (own_weight + factor * total)


def layer_kernel(
    hand, new_len, res_len, queries, own_kv, resident, caches, weight,
    attended, arrived_out, meta_all,
    own, other, packed, arrived, res, held, meta_send, q3, eq3, own_k, own_v, own_s, selector, rows3, entry_out,
    staged, parts,
    own_sem, pair_send, pair_recv, send, recv, stay, meta_s, meta_r, res_sem, out_sem, load, rs_send, rs_recv, ag_send, ag_recv,
):
    rep, tp = lax.axis_index("rep"), lax.axis_index("tp")
    parity = tp % 2
    partner = tp + 1 - 2 * parity
    count, half, width = own.shape
    row_count = res.shape[0]
    peers = len(REP_STEPS)
    mine = pl.ds(pl.multiple_of(parity * width, width), width)
    theirs = pl.ds(pl.multiple_of((1 - parity) * width, width), width)
    own_load = pltpu.make_async_copy(caches.at[:, 0, :, mine], own, own_sem)
    own_load.start()
    res_loads = []
    part_rows = row_count // RES_PARTS
    for k in range(RES_PARTS):
        rows = pl.ds(k * part_rows, part_rows)
        copy = pltpu.make_async_copy(resident.at[rows], res.at[rows], res_sem.at[k])
        copy.start()
        res_loads.append(copy)

    barrier = pltpu.get_barrier_semaphore()
    for step in REP_STEPS:
        pl.semaphore_signal(barrier, inc=1, device_id=(rep_at(rep, step, -1), tp), device_id_type=MESH)
    for step in TP_STEPS:
        pl.semaphore_signal(barrier, inc=1, device_id=(rep, tp_at(tp, step, -1)), device_id_type=MESH)

    targets = [hand[0, i, 0] for i in range(count)]

    def slot_picks(group):
        seen, first, second = jnp.int32(0), jnp.int32(0), jnp.int32(0)
        for i in range(count):
            hit = targets[i] == group
            first = jnp.where(hit & (seen == 0), i, first)
            second = jnp.where(hit & (seen == 1), i, second)
            seen = seen + hit.astype(jnp.int32)
        return first, second, seen

    def code_of(pick, filled):
        return jnp.where(filled, hand[0, pick, 1] + LEN_UNIT * new_len[0, pick], NO_ROW)

    picks = []
    for k, step in enumerate(REP_STEPS + [(0, 0, 0)]):
        first, second, seen = slot_picks(rep_at(rep, step, 1))
        picks.append((first, second))
        meta_send[k, 0:8, :] = jnp.full((8, HEAD), code_of(first, seen > 0), jnp.int32)
        meta_send[k, 8:16, :] = jnp.full((8, HEAD), code_of(second, seen > 1), jnp.int32)
    meta_all[rep] = meta_send[peers]
    pl.semaphore_wait(barrier, len(REP_STEPS) + len(TP_STEPS))

    pair = pltpu.make_async_remote_copy(
        src_ref=caches.at[:, 0, :, theirs], dst_ref=other, send_sem=pair_send, recv_sem=pair_recv,
        device_id=(rep, partner), device_id_type=MESH,
    )
    pair.start()
    metas = []
    for k, step in enumerate(REP_STEPS):
        copy = pltpu.make_async_remote_copy(
            src_ref=meta_send.at[k], dst_ref=meta_all.at[rep], send_sem=meta_s.at[k], recv_sem=meta_r.at[k],
            device_id=(rep_at(rep, step, 1), tp), device_id_type=MESH,
        )
        copy.start()
        metas.append(copy)

    slots = pl.ds(rep * CAP, CAP)
    bulk = [[], []]

    def send_phase(phase, from_ref):
        part = parity if phase == 0 else 1 - parity
        tokens = pl.ds(pl.multiple_of(part * half, half), half)
        for k, step in enumerate(REP_STEPS):
            packed[phase, k, 0] = from_ref[picks[k][0]]
            packed[phase, k, 1] = from_ref[picks[k][1]]
            copy = pltpu.make_async_remote_copy(
                src_ref=packed.at[phase, k], dst_ref=arrived.at[slots, tokens, :],
                send_sem=send.at[phase, k], recv_sem=recv.at[phase, k],
                device_id=(rep_at(rep, step, 1), tp), device_id_type=MESH,
            )
            copy.start()
            bulk[phase].append(copy)
        packed[phase, peers, 0] = from_ref[picks[peers][0]]
        packed[phase, peers, 1] = from_ref[picks[peers][1]]
        copy = pltpu.make_async_copy(packed.at[phase, peers], arrived.at[slots, tokens, :], stay.at[phase])
        copy.start()
        bulk[phase].append(copy)

    own_load.wait()
    send_phase(0, own)

    tp_steps = TP_STEPS + [(0, 0)]
    block = held.shape[2]
    w_loads = []
    for k, step in enumerate(tp_steps):
        at = pl.multiple_of(tp_at(tp, step, 1) * block, block)
        copy = pltpu.make_async_copy(weight.at[:, pl.ds(at, block)], held.at[k], load.at[k])
        copy.start()
        w_loads.append(copy)

    heads = queries.shape[1] // HEAD
    for j in range(heads):
        q3[:, j, :] = queries[:, j * HEAD:(j + 1) * HEAD].astype(jnp.float32)
    pairs = row_count * heads
    q_rows = q3[...].reshape(pairs, HEAD)
    own_now = own_kv[...].astype(jnp.float32)
    own_rows = jnp.broadcast_to(own_now[:, None, :], (row_count, heads, width)).reshape(pairs, width)

    low_col = iota((2 * heads, 1), 0) < heads

    def resident_pair(i, carry):
        a, b = 2 * i, 2 * i + 1
        limits = jnp.where(low_col, res_len[0, a], res_len[0, b])
        peak, total, acc = attend_pair(
            q3[pl.ds(a, 2)].reshape(2 * heads, HEAD), res[a], res[b], limits
        )
        at = pl.ds(pl.multiple_of(i * 2 * heads, 2 * heads), 2 * heads)
        rows3[0, at, :] = jnp.broadcast_to(peak, acc.shape)
        rows3[1, at, :] = jnp.broadcast_to(total, acc.shape)
        rows3[2, at, :] = acc
        return carry

    for k in range(RES_PARTS):
        res_loads[k].wait()
        lax.fori_loop(k * part_rows // 2, (k + 1) * part_rows // 2, resident_pair, 0)
    row_score = jnp.sum(q_rows * own_rows[:, :HEAD], axis=1, keepdims=True) * SCALE
    rows3[2] = combine(rows3[0], rows3[1], rows3[2], row_score, own_rows[:, HEAD:])

    for copy in metas:
        copy.wait_recv()
    codes = meta_all[...].reshape(pairs, HEAD)
    row_of = codes % LEN_UNIT
    lane, sub = iota((pairs, HEAD), 1), iota((pairs, HEAD), 0)
    lanes_rows = HEAD // heads
    for b in range(row_count // lanes_rows):
        hit = (row_of == b * lanes_rows + lane // heads) & (lane % heads == sub % heads)
        selector[:, b * HEAD:(b + 1) * HEAD] = hit.astype(jnp.float32).astype(jnp.bfloat16)
    picked = jnp.dot(selector[...], q_rows.astype(jnp.bfloat16), preferred_element_type=jnp.float32)
    eq3[...] = picked
    picked_kv = jnp.dot(selector[...], own_rows.astype(jnp.bfloat16), preferred_element_type=jnp.float32)
    own_s[...] = jnp.broadcast_to(
        jnp.sum(picked * picked_kv[:, :HEAD], axis=1, keepdims=True) * SCALE, (pairs, HEAD)
    )
    own_v[...] = picked_kv[:, HEAD:]
    own_k[...] = (codes // LEN_UNIT).astype(jnp.int32)
    taken = contract_first(selector[...], jnp.ones((pairs, HEAD), jnp.bfloat16))

    pair.wait_recv()
    send_phase(1, other)

    out_copies = []
    order = [(peers, rep)] + [(k, rep_at(rep, step, -1)) for k, step in enumerate(REP_STEPS)]
    for k, group in order:
        for phase in (0, 1):
            if k == peers:
                bulk[phase][k].wait()
            else:
                bulk[phase][k].wait_recv()
        here = pl.ds(group * CAP, CAP)
        copy = pltpu.make_async_copy(arrived.at[here], arrived_out.at[here], out_sem.at[k])
        copy.start()
        out_copies.append(copy)
        at = pl.ds(pl.multiple_of(group * CAP * heads, CAP * heads), CAP * heads)
        limits = own_k[at, :][:, 0:1]
        peak, total, acc = attend_pair(eq3[at, :], arrived[group * CAP], arrived[group * CAP + 1], limits)
        entry_out[at, :] = combine(peak, total, acc, own_s[at, :], own_v[at, :]).astype(jnp.bfloat16)

    moved = contract_first(selector[...], entry_out[...])
    q3[...] = jnp.where(taken > 0.5, moved, rows3[2]).reshape(row_count, heads, HEAD)
    attention = jnp.concatenate([q3[:, j, :] for j in range(heads)], axis=1).astype(jnp.bfloat16)

    last = len(TP_STEPS)
    scatter = []
    for k, step in enumerate(TP_STEPS):
        w_loads[k].wait()
        staged[k] = jnp.dot(attention, held[k], preferred_element_type=jnp.float32).astype(staged.dtype)
        copy = pltpu.make_async_remote_copy(
            src_ref=staged.at[k], dst_ref=parts.at[k], send_sem=rs_send.at[k], recv_sem=rs_recv.at[k],
            device_id=(rep, tp_at(tp, step, 1)), device_id_type=MESH,
        )
        copy.start()
        scatter.append(copy)
    w_loads[last].wait()
    total = jnp.dot(attention, held[last], preferred_element_type=jnp.float32)
    for k in range(last):
        scatter[k].wait_recv()
        total = total + parts[k].astype(jnp.float32)
    columns = pl.ds(pl.multiple_of(tp * block, block), block)
    attended[:, columns] = total.astype(attended.dtype)
    gather = []
    for k, step in enumerate(TP_STEPS):
        copy = pltpu.make_async_remote_copy(
            src_ref=attended.at[:, columns], dst_ref=attended.at[:, columns], send_sem=ag_send.at[k], recv_sem=ag_recv.at[k],
            device_id=(rep, tp_at(tp, step, 1)), device_id_type=MESH,
        )
        copy.start()
        gather.append(copy)
    pair.wait_send()
    for copy in metas + bulk[0][:peers] + bulk[1][:peers] + scatter:
        copy.wait_send()
    for copy in out_copies + gather:
        copy.wait()


def run_layer(queries, new_token_kv, resident_cache, resident_lengths, new_caches, new_lengths, handoff, out_weight):
    count, _, half, wide = new_caches.shape
    width = wide // 2
    groups, shares = lax.axis_size("rep"), lax.axis_size("tp")
    entries = groups * CAP
    rows, depth = queries.shape
    heads = depth // HEAD
    pairs = rows * heads
    columns = out_weight.shape[1]
    block = columns // shares
    peers, tp_peers = len(REP_STEPS), len(TP_STEPS)
    kind = new_caches.dtype
    dma = pltpu.SemaphoreType.DMA
    vmem = pl.BlockSpec(memory_space=pltpu.VMEM)
    smem = pl.BlockSpec(memory_space=pltpu.SMEM)
    far = pl.BlockSpec(memory_space=pl.ANY)
    return pl.pallas_call(
        layer_kernel,
        out_shape=(
            jax.ShapeDtypeStruct((rows, columns), kind),
            jax.ShapeDtypeStruct((entries, 2 * half, width), kind),
            jax.ShapeDtypeStruct((groups, CAP * heads, HEAD), jnp.int32),
        ),
        in_specs=[smem, smem, smem, vmem, vmem, far, far, far],
        out_specs=(vmem, far, vmem),
        scratch_shapes=[
            pltpu.VMEM((count, half, width), kind),
            pltpu.VMEM((count, half, width), kind),
            pltpu.VMEM((2, groups, CAP, half, width), kind),
            pltpu.VMEM((entries, 2 * half, width), kind),
            pltpu.VMEM(resident_cache.shape, kind),
            pltpu.VMEM((shares, depth, block), kind),
            pltpu.VMEM((groups, CAP * heads, HEAD), jnp.int32),
            pltpu.VMEM((rows, heads, HEAD), jnp.float32),
            pltpu.VMEM((entries * heads, HEAD), jnp.float32),
            pltpu.VMEM((entries * heads, HEAD), jnp.int32),
            pltpu.VMEM((entries * heads, HEAD), jnp.float32),
            pltpu.VMEM((entries * heads, HEAD), jnp.float32),
            pltpu.VMEM((entries * heads, pairs), kind),
            pltpu.VMEM((3, pairs, HEAD), jnp.float32),
            pltpu.VMEM((entries * heads, HEAD), kind),
            pltpu.VMEM((tp_peers, rows, block), kind),
            pltpu.VMEM((tp_peers, rows, block), kind),
            dma, dma, dma, dma((2, peers)), dma((2, peers)), dma((2,)), dma((peers,)), dma((peers,)),
            dma((RES_PARTS,)), dma((peers + 1,)), dma((shares,)),
            dma((tp_peers,)), dma((tp_peers,)), dma((tp_peers,)), dma((tp_peers,)),
        ],
        compiler_params=pltpu.CompilerParams(
            collective_id=0, has_side_effects=True, vmem_limit_bytes=48 * 2**20
        ),
        name="layer",
    )(handoff, new_lengths, resident_lengths, queries, new_token_kv, resident_cache, new_caches, out_weight)


def install_kernel(res_len, own_kv, meta, arrived, resident, updated, buf, own_now, codes, entry, limit, meta_sem, get, put):
    rows, tokens, width = buf.shape
    groups = meta.shape[0]
    heads = meta.shape[1] // CAP
    capacity = arrived.shape[1]
    fetch = pltpu.make_async_copy(meta, codes, meta_sem)
    fetch.start()
    own_now[...] = own_kv[...].astype(jnp.float32)

    def clear(r, carry):
        entry[r] = -1
        limit[r] = res_len[0, jnp.minimum(r, rows - 1)]
        return carry

    lax.fori_loop(0, rows + 1, clear, 0)
    fetch.wait()
    for g in range(groups):
        for s in range(CAP):
            code = codes[g, s * heads, 0]
            row = code % LEN_UNIT
            entry[row] = g * CAP + s
            limit[row] = code // LEN_UNIT

    def get_new(r):
        return pltpu.make_async_copy(arrived.at[entry[r]], buf.at[r, pl.ds(0, capacity), :], get.at[r])

    def get_old(r):
        return pltpu.make_async_copy(resident.at[r], buf.at[r], get.at[r])

    def start(r, carry):
        @pl.when(entry[r] >= 0)
        def _():
            get_new(r).start()

        @pl.when(entry[r] < 0)
        def _():
            get_old(r).start()
        return carry

    lax.fori_loop(0, rows, start, 0)

    def patch(r, carry):
        length = limit[r]
        token = own_now[pl.ds(r, 1), :]

        @pl.when(entry[r] >= 0)
        def _():
            get_new(r).wait()
            at = iota((capacity, width), 0)
            kept = jnp.where(at < length, buf[r, 0:capacity, :].astype(jnp.float32), 0.0)
            buf[r, 0:capacity, :] = jnp.where(at == length, token, kept).astype(buf.dtype)
            at = iota((tokens - capacity, width), 0) + capacity
            buf[r, capacity:tokens, :] = jnp.where(at == length, token, 0.0).astype(buf.dtype)

        @pl.when(entry[r] < 0)
        def _():
            get_old(r).wait()
            first = pl.multiple_of((length // 16) * 16, 16)
            here = buf[r, pl.ds(first, 16), :].astype(jnp.float32)
            at = iota((16, width), 0) + first
            buf[r, pl.ds(first, 16), :] = jnp.where(at == length, token, here).astype(buf.dtype)

        pltpu.make_async_copy(buf.at[r], updated.at[r], put.at[r]).start()
        return carry

    lax.fori_loop(0, rows, patch, 0)

    def finish(r, carry):
        pltpu.make_async_copy(buf.at[r], updated.at[r], put.at[r]).wait()
        return carry

    lax.fori_loop(0, rows, finish, 0)


def install(resident_lengths, new_token_kv, meta, arrived, resident_cache):
    rows, _, width = resident_cache.shape
    dma = pltpu.SemaphoreType.DMA
    vmem = pl.BlockSpec(memory_space=pltpu.VMEM)
    smem = pl.BlockSpec(memory_space=pltpu.SMEM)
    far = pl.BlockSpec(memory_space=pl.ANY)
    return pl.pallas_call(
        install_kernel,
        out_shape=jax.ShapeDtypeStruct(resident_cache.shape, resident_cache.dtype),
        in_specs=[smem, vmem, far, far, far],
        out_specs=far,
        scratch_shapes=[
            pltpu.VMEM(resident_cache.shape, resident_cache.dtype),
            pltpu.VMEM((rows, width), jnp.float32),
            pltpu.SMEM(meta.shape, jnp.int32),
            pltpu.SMEM((rows + 1,), jnp.int32),
            pltpu.SMEM((rows + 1,), jnp.int32),
            dma, dma((rows,)), dma((rows,)),
        ],
        compiler_params=pltpu.CompilerParams(vmem_limit_bytes=48 * 2**20),
        name="install",
    )(resident_lengths, new_token_kv, meta, arrived, resident_cache)


def body(
    queries,
    new_token_kv,
    resident_cache,
    resident_lengths,
    new_caches,
    new_lengths,
    handoff,
    out_weight,
):
    attended, arrived, meta = run_layer(
        queries, new_token_kv, resident_cache, resident_lengths, new_caches, new_lengths, handoff, out_weight
    )
    updated = install(resident_lengths, new_token_kv, meta, arrived, resident_cache)
    return (attended, updated)


def solution(mesh):
    placed = (
        P("rep", "tp"),
        P("rep", "tp"),
        P("rep", None, "tp"),
        P("rep", None),
        P("rep", "tp", None, None),
        P("rep", None),
        P("rep", None, None),
        P("tp", None),
    )
    return jax.shard_map(
        body,
        mesh=mesh,
        in_specs=placed,
        out_specs=(P("rep", None), P("rep", None, "tp")),
        check_vma=False,
    )
```

time: 260 us -> 99.8 us (0.38)
  the two profiles are of different devices: /device:TPU:96 before, /device:TPU:32 now
where the time goes in v2:
time: 99.8 us; the launch traced here: 99.5 us
  Pallas kernels  90.6 us (91%)
  local copies, waits for them, and re-layouts  8.19 us (8%)
    pallas_call x1, Pallas kernels, run_layer(): pl.pallas_call(layer_kernel, out_shape=(jax.ShapeDtypeStruct((rows, colum...  77.5 us
    pallas_call x1, Pallas kernels, install(): pl.pallas_call(install_kernel, out_shape=jax.ShapeDtypeStruct(resident_ca...  13.1 us
    unnamed x16, local copies, waits for them, and re-layouts  8.19 us

profile of v2, /device:TPU:32, one launch (start us, length us, event | category | flops | bytes accessed | tf_op | source)
XLA Modules:
  0.0 99.5 jit_solution(10824299960348898857)
XLA Ops:
  0.6 0.8 copy.10.hand
  1.4 0.0 copy-start.1
  1.4 1.6 %copy-done.1 = bf16[16,1,128,512]{3,2,1,0:T(8,128)(2,1)S(1)} copy-done((bf16[16,1,128,512]{3,2,1,0:T(8,128)(2,1)S(1)}, bf16[16,1,128,512]{3,2,1,0:T(8,128)(2,1)}, u32[]{:S(2)}) %copy-start.1) | copy-done | bytes 2097176
  3.0 0.0 copy-start.2
  3.0 0.8 copy-done.2
  3.8 0.0 copy-start.3
  3.8 0.7 copy-done.3
  4.5 0.0 copy-start.5
  4.5 0.7 copy-done.5
  5.2 0.0 copy-start.6
  5.2 0.7 copy-done.6
  5.8 0.0 copy-start.4
  5.8 77.5 %layer.1 = (bf16[32,8192]{1,0:T(8,128)(2,1)S(1)}, bf16[32,256,256]{2,1,0:T(8,128)(2,1)}, s32[16,16,128]{2,1,0:T(8,128)S(1)}) custom-call(s32[1,16,2]{2,1,0:T(8,128)S(1)} %copy.10.hand, s32[1,16]{1,0:T(1,128)S(1)} %copy-done.6, s32[1,32]{1,0:T(1,128)S(1)} %copy-done.5, bf16[32,1024]{1,0:T(8,128)(2,1)S(1)} %copy-done.2, bf16[32,256]{1,0:T(8,128)(2,1)S(1)} %copy-done.3, ...), custom_call_target="tpu_custom_call" | custom-call | tf_op jit(solution)/shard_map/layer/pallas_call | solution.py:296
  83.4 0.0 copy-done.4
  83.4 0.0 copy-start
  83.4 2.2 %copy-done = bf16[32,256,256]{2,1,0:T(8,128)(2,1)S(1)} copy-done((bf16[32,256,256]{2,1,0:T(8,128)(2,1)S(1)}, bf16[32,256,256]{2,1,0:T(8,128)(2,1)}, u32[]{:S(2)}) %copy-start) | copy-done | bytes 4194328
  85.6 13.1 %install.1 = bf16[32,384,256]{2,1,0:T(8,128)(2,1)} custom-call(s32[1,32]{1,0:T(1,128)S(1)} %copy-done.5, bf16[32,256]{1,0:T(8,128)(2,1)S(1)} %copy-done.4, s32[16,16,128]{2,1,0:T(8,128)S(1)} %get-tuple-element.6.meta, bf16[32,256,256]{2,1,0:T(8,128)(2,1)S(1)} %copy-done, bf16[32,384,256]{2,1,0:T(8,128)(2,1)} %resident.3), custom_call_target="tpu_custom_call" | custom-call | tf_op jit(solution)/shard_map/install/pallas_call | solution.py:414
  98.7 0.8 copy.12
Async XLA Ops:
  1.4 1.6 %copy-start.1 = (bf16[16,1,128,512]{3,2,1,0:T(8,128)(2,1)S(1)}, bf16[16,1,128,512]{3,2,1,0:T(8,128)(2,1)}, u32[]{:S(2)}) copy-start(bf16[16,1,128,512]{3,2,1,0:T(8,128)(2,1)} %caches.1) | copy-start | bytes 6291460
  3.0 0.8 copy-start.2
  3.8 0.7 copy-start.3
  4.5 0.7 copy-start.5
  5.2 0.7 copy-start.6
  5.8 77.5 %copy-start.4 = (bf16[32,256]{1,0:T(8,128)(2,1)S(1)}, bf16[32,256]{1,0:T(8,128)(2,1)}, u32[]{:S(2)}) copy-start(bf16[32,256]{1,0:T(8,128)(2,1)} %own_kv.3) | copy-start | bytes 49156
  83.4 2.2 %copy-start = (bf16[32,256,256]{2,1,0:T(8,128)(2,1)S(1)}, bf16[32,256,256]{2,1,0:T(8,128)(2,1)}, u32[]{:S(2)}) copy-start(bf16[32,256,256]{2,1,0:T(8,128)(2,1)} %get-tuple-element.7.arrived) | copy-start | bytes 12582916

commit v3 on v2

v3 whole, which is shorter than its diff:
```python
import functools

import jax
import jax.numpy as jnp
from jax import lax
from jax.experimental import pallas as pl
from jax.experimental.pallas import tpu as pltpu
from jax.sharding import PartitionSpec as P

HEAD = 128
CAP = 2
NEG_FILL = -1e30
SCALE = HEAD ** (-0.5)
MESH = pl.DeviceIdType.MESH
NO_ROW = 32
LEN_UNIT = 64
RES_PARTS = 4
VMEM_BYTES = 63 * 2**20
CHUNKS = 4
PORTIONS = (32, 32, 24, 20, 10)
RES_EARLY = 2

REP_STEPS = [
    (1, 1, 0), (0, 3, 0), (1, 2, 0), (0, 1, 1), (1, 3, 1), (1, 0, 0), (0, 2, 1), (1, 1, 1),
    (0, 3, 1), (1, 2, 1), (0, 1, 0), (1, 3, 0), (1, 0, 1), (0, 2, 0), (0, 0, 1),
]
TP_STEPS = [(h, x) for x in (2, 1, 3, 0) for h in (1, 0) if (h, x) != (0, 0)]
X_STEPS = (2, 1, 3)


def rep_at(rep, step, sign):
    y, z, c = rep // 8, (rep // 2) % 4, rep % 2
    dy, dz, dc = step
    return ((y + dy) % 2) * 8 + ((z + sign * dz + 4) % 4) * 2 + (c + dc) % 2


def tp_at(tp, step, sign):
    h, x = tp // 4, tp % 4
    dh, dx = step
    return ((h + dh) % 2) * 4 + (x + sign * dx + 4) % 4


def iota(shape, dim):
    return lax.broadcasted_iota(jnp.int32, shape, dim)


def contract_last(a, b):
    return lax.dot_general(a, b, (((1,), (1,)), ((), ())), preferred_element_type=jnp.float32)


def contract_first(a, b):
    return lax.dot_general(a, b, (((0,), (0,)), ((), ())), preferred_element_type=jnp.float32)


def attend_pair(query_pair, kv_a, kv_b, limits):
    low = iota(query_pair.shape, 0) < 8
    zero = jnp.zeros_like(query_pair)
    blocks = jnp.concatenate([jnp.where(low, query_pair, zero), jnp.where(low, zero, query_pair)], axis=1)
    keys = jnp.concatenate([kv_a[:, :HEAD], kv_b[:, :HEAD]], axis=1)
    values = jnp.concatenate([kv_a[:, HEAD:], kv_b[:, HEAD:]], axis=1)
    scores = contract_last(blocks.astype(jnp.bfloat16), keys) * SCALE
    allowed = iota(scores.shape, 1) < limits
    peak = jnp.max(jnp.where(allowed, scores, NEG_FILL), axis=1, keepdims=True)
    weights = jnp.where(allowed, jnp.exp(jnp.where(allowed, scores, peak) - peak), 0.0).astype(jnp.bfloat16)
    total = jnp.sum(weights.astype(jnp.float32), axis=1, keepdims=True)
    both = jnp.dot(weights, values, preferred_element_type=jnp.float32)
    return peak, total, jnp.where(low, both[:, :HEAD], both[:, HEAD:])


def combine(peak, total, acc, own_score, own_value):
    top = jnp.maximum(peak, own_score)
    own_weight, factor = jnp.exp(own_score - top), jnp.exp(peak - top)
    return (own_weight * own_value + factor * acc) / (own_weight + factor * total)


def layer_kernel(
    hand, new_len, res_len, queries, own_kv, resident, caches, weight,
    attended, arrived, table,
    meta_send, meta_all, own, theirs, other0, other1, other2, other3, packed, packed2, res, held, q3, query_out, query_in, query_by, acc_by, note_by, part_out, part_in, note_out, note_in,
    selector, rows3, staged, parts, sums,
    own_sem, pair_send, pair_recv, send, recv, stay, meta_s, meta_r, q_s, q_r, p_s, p_r, n_s, n_r, res_sem, load,
    rs_send, rs_recv, swap_send, swap_recv, ag_send, ag_recv,
):
    rep, tp = lax.axis_index("rep"), lax.axis_index("tp")
    parity = tp % 2
    partner = tp + 1 - 2 * parity
    count, half, width = own.shape
    row_count = res.shape[0]
    peers = len(REP_STEPS)
    mine = pl.ds(pl.multiple_of(parity * width, width), width)
    away = pl.ds(pl.multiple_of((1 - parity) * width, width), width)
    own_loads = [
        pltpu.make_async_copy(caches.at[:, 0, :, mine], own, own_sem.at[0]),
        pltpu.make_async_copy(caches.at[:, 0, :, away], theirs, own_sem.at[1]),
    ]
    for copy in own_loads:
        copy.start()
    res_loads = []
    part_rows = row_count // RES_PARTS
    for k in range(RES_PARTS):
        rows = pl.ds(k * part_rows, part_rows)
        copy = pltpu.make_async_copy(resident.at[rows], res.at[rows], res_sem.at[k])
        copy.start()
        res_loads.append(copy)

    barrier = pltpu.get_barrier_semaphore()
    for step in REP_STEPS:
        for to in (tp, partner):
            pl.semaphore_signal(barrier, inc=1, device_id=(rep_at(rep, step, -1), to), device_id_type=MESH)
    for step in TP_STEPS:
        pl.semaphore_signal(barrier, inc=1, device_id=(rep, tp_at(tp, step, -1)), device_id_type=MESH)

    targets = [hand[0, 0, i] for i in range(count)]

    def slot_picks(group):
        seen, first, second = jnp.int32(0), jnp.int32(0), jnp.int32(0)
        for i in range(count):
            hit = targets[i] == group
            first = jnp.where(hit & (seen == 0), i, first)
            second = jnp.where(hit & (seen == 1), i, second)
            seen = seen + hit.astype(jnp.int32)
        return first, second, seen

    def code_of(pick, filled):
        return jnp.where(filled, hand[0, 1, pick] + LEN_UNIT * new_len[0, pick], NO_ROW)

    all_steps = REP_STEPS + [(0, 0, 0)]
    picks = []
    code_lane = iota((1, HEAD), 1)
    for k, step in enumerate(all_steps):
        first, second, seen = slot_picks(rep_at(rep, step, 1))
        picks.append((first, second))
        meta_send[k] = jnp.where(code_lane < HEAD // CAP, code_of(first, seen > 0), code_of(second, seen > 1))
    meta_all[rep] = meta_send[peers]
    pl.semaphore_wait(barrier, 2 * len(REP_STEPS) + len(TP_STEPS))

    metas = []
    for k, step in enumerate(REP_STEPS):
        copy = pltpu.make_async_remote_copy(
            src_ref=meta_send.at[k], dst_ref=meta_all.at[rep], send_sem=meta_s.at[k], recv_sem=meta_r.at[k],
            device_id=(rep_at(rep, step, 1), tp), device_id_type=MESH,
        )
        copy.start()
        metas.append(copy)
    pairs_sent = []
    others = (other0, other1, other2, other3)
    span = half // CHUNKS

    def send_chunk():
        c = len(pairs_sent)
        tokens = pl.ds(c * span, span)
        copy = pltpu.make_async_remote_copy(
            src_ref=caches.at[:, 0, tokens, away], dst_ref=others[c],
            send_sem=pair_send.at[c], recv_sem=pair_recv.at[c], device_id=(rep, partner), device_id_type=MESH,
        )
        copy.start()
        pairs_sent.append(copy)

    slots = pl.ds(rep * CAP, CAP)
    bulk = []
    pieces = [(None, k) for k in range(peers + 1)] + [(c, k) for c in range(CHUNKS) for k in range(peers + 1)]

    def issue(units):
        while units > 0 and len(bulk) < len(pieces):
            c, k = pieces[len(bulk)]
            first, second = picks[k]
            if c is None:
                if k == 0:
                    own_loads[0].wait()
                packed[k, 0] = own[first]
                packed[k, 1] = own[second]
                source, sems = packed.at[k], 0
                tokens = pl.ds(pl.multiple_of(parity * half, half), half)
                units -= CHUNKS
            else:
                if k == 0:
                    pairs_sent[c].wait_recv()
                packed2[c, k, 0] = others[c][first]
                packed2[c, k, 1] = others[c][second]
                source, sems = packed2.at[c, k], c + 1
                tokens = pl.ds(pl.multiple_of((1 - parity) * half + c * span, span), span)
                units -= 1
            if k < peers:
                copy = pltpu.make_async_remote_copy(
                    src_ref=source, dst_ref=arrived.at[slots, tokens, :], send_sem=send.at[sems, k], recv_sem=recv.at[sems, k],
                    device_id=(rep_at(rep, all_steps[k], 1), tp), device_id_type=MESH,
                )
            else:
                copy = pltpu.make_async_copy(source, arrived.at[slots, tokens, :], stay.at[sems])
            copy.start()
            bulk.append(copy)

    send_chunk()
    issue(PORTIONS[0])

    heads = queries.shape[1] // HEAD
    for j in range(heads):
        q3[:, j, :] = queries[:, j * HEAD:(j + 1) * HEAD].astype(jnp.float32)
    pairs = row_count * heads
    tile = CAP * heads
    q_rows = q3[...].reshape(pairs, HEAD)
    own_now = own_kv[...].astype(jnp.float32)
    own_rows = jnp.broadcast_to(own_now[:, None, :], (row_count, heads, width)).reshape(pairs, width)

    for copy in metas:
        copy.wait_recv()
    codes = meta_all[...]
    codes = jnp.stack(
        [jnp.broadcast_to(codes[:, :, at:at + 1], (peers + 1, heads, HEAD)) for at in range(0, HEAD, HEAD // CAP)], axis=1
    ).reshape(pairs, HEAD)
    row_of = codes % LEN_UNIT
    lane, sub = iota((pairs, HEAD), 1), iota((pairs, HEAD), 0)
    lanes_rows = HEAD // heads
    for b in range(row_count // lanes_rows):
        hit = (row_of == b * lanes_rows + lane // heads) & (lane % heads == sub % heads)
        selector[:, b * HEAD:(b + 1) * HEAD] = hit.astype(jnp.float32).astype(jnp.bfloat16)
    picked = jnp.dot(selector[...], q_rows.astype(jnp.bfloat16), preferred_element_type=jnp.float32)
    query_out[...] = picked.astype(jnp.bfloat16).reshape(peers + 1, tile, HEAD)
    query_in[0, rep] = query_out[rep]
    asks = []
    for k, step in enumerate(all_steps):
        group = rep_at(rep, step, 1)
        for w, to in ((0, tp), (1, partner)):
            if k == peers and w == 0:
                continue
            copy = pltpu.make_async_remote_copy(
                src_ref=query_out.at[group], dst_ref=query_in.at[w, rep], send_sem=q_s.at[w, k], recv_sem=q_r.at[w, k],
                device_id=(group, to), device_id_type=MESH,
            )
            copy.start()
            asks.append(copy)
    send_chunk()
    send_chunk()
    issue(PORTIONS[1])

    low_col = iota((tile, 1), 0) < heads

    def resident_pair(i, carry):
        a, b = 2 * i, 2 * i + 1
        limits = jnp.where(low_col, res_len[0, a], res_len[0, b])
        peak, total, acc = attend_pair(q3[pl.ds(a, 2)].reshape(tile, HEAD), res[a], res[b], limits)
        at = pl.ds(pl.multiple_of(i * tile, tile), tile)
        rows3[0, at, :] = jnp.broadcast_to(peak, acc.shape)
        rows3[1, at, :] = jnp.broadcast_to(total, acc.shape)
        rows3[2, at, :] = acc
        return carry

    def resident_part(k):
        res_loads[k].wait()
        lax.fori_loop(k * part_rows // 2, (k + 1) * part_rows // 2, resident_pair, 0)

    for k in range(RES_EARLY):
        resident_part(k)

    for copy in asks:
        copy.wait_recv()
    own_loads[1].wait()
    query_by[...] = query_in[...].astype(jnp.float32).reshape(query_by.shape)

    for i in range(count):
        at = targets[i] * CAP + sum([(targets[n] == targets[i]).astype(jnp.int32) for n in range(i)], jnp.int32(0))
        asked = jnp.concatenate([query_by[0, at], query_by[1, at]], axis=0)
        peak, total, acc = attend_pair(asked, own[i], theirs[i], new_len[0, i] - half * parity)
        acc_by[i] = acc
        peak, total = jnp.broadcast_to(peak, acc.shape), jnp.broadcast_to(total, acc.shape)
        note_by[i] = jnp.where(iota(acc.shape, 1) % 2 == 0, peak, total)
    note_lane, note_sub = iota((heads, HEAD), 1), iota((heads, HEAD), 0)
    answers = []
    for k, step in enumerate(all_steps):
        first, second = picks[k]
        group = rep_at(rep, step, 1)
        for w, to in ((0, tp), (1, partner)):
            of = slice(w * heads, (w + 1) * heads)
            both = jnp.concatenate([acc_by[first][of], acc_by[second][of]], axis=0).astype(part_out.dtype)
            note = jnp.where(note_lane % 4 < 2, note_by[first][of], note_by[second][of])
            note = jnp.sum(jnp.where(note_lane // 4 == note_sub, note, 0.0), axis=0, keepdims=True)
            if k == peers and w == 0:
                part_in[0, rep] = both
                note_in[0, rep] = note
                continue
            part_out[w, k] = both
            note_out[w, k] = note
            for source, target, out_sem, in_sem in ((part_out, part_in, p_s, p_r), (note_out, note_in, n_s, n_r)):
                copy = pltpu.make_async_remote_copy(
                    src_ref=source.at[w, k], dst_ref=target.at[w, rep], send_sem=out_sem.at[w, k], recv_sem=in_sem.at[w, k],
                    device_id=(group, to), device_id_type=MESH,
                )
                copy.start()
                answers.append(copy)
    send_chunk()
    issue(PORTIONS[2])
    here = tp % 4
    block = held.shape[2]
    w_loads = []
    for k, step in enumerate(X_STEPS + (0,)):
        at = pl.multiple_of(((here + step) % 4) * block, block)
        copy = pltpu.make_async_copy(weight.at[:, pl.ds(at, block)], held.at[k], load.at[k])
        copy.start()
        w_loads.append(copy)

    for k in range(RES_EARLY, RES_PARTS):
        resident_part(k)
    row_score = jnp.sum(q_rows * own_rows[:, :HEAD], axis=1, keepdims=True) * SCALE
    rows3[2] = combine(rows3[0], rows3[1], rows3[2], row_score, own_rows[:, HEAD:])
    picked_kv = jnp.dot(selector[...], own_rows.astype(jnp.bfloat16), preferred_element_type=jnp.float32)
    entry_score = jnp.sum(picked * picked_kv[:, :HEAD], axis=1, keepdims=True) * SCALE
    taken = contract_first(selector[...], jnp.ones((pairs, HEAD), jnp.bfloat16))
    entry_of = (sub // heads + 1).astype(jnp.float32)
    notes = jnp.where(lane == 0, entry_of, jnp.where(lane == 1, (codes // LEN_UNIT).astype(jnp.float32), 0.0))
    table[...] = contract_first(notes.astype(jnp.bfloat16), selector[...])[0:8, :].astype(jnp.int32)

    for copy in answers:
        copy.wait_recv()
    peaks, totals, accs = [], [], []
    cell, cell_sub = iota((peers + 1, heads, HEAD), 2), iota((peers + 1, heads, HEAD), 1)
    for w in range(CAP):
        accs.append(part_in[w].astype(jnp.float32).reshape(pairs, HEAD))
        note = jnp.broadcast_to(note_in[w], cell.shape)

        def column(at):
            found = jnp.sum(jnp.where(cell == 4 * cell_sub + at, note, 0.0), axis=2, keepdims=True)
            return jnp.broadcast_to(found, cell.shape)

        peaks.append(jnp.stack([column(0), column(2)], axis=1).reshape(pairs, HEAD))
        totals.append(jnp.stack([column(1), column(3)], axis=1).reshape(pairs, HEAD))
    top = jnp.maximum(jnp.maximum(peaks[0], peaks[1]), entry_score)
    own_weight = jnp.exp(entry_score - top)
    factors = [jnp.exp(peak - top) for peak in peaks]
    above = own_weight * picked_kv[:, HEAD:] + factors[0] * accs[0] + factors[1] * accs[1]
    below = own_weight + factors[0] * totals[0] + factors[1] * totals[1]
    moved = contract_first(selector[...], (above / below).astype(jnp.bfloat16))
    q3[...] = jnp.where(taken > 0.5, moved, rows3[2]).reshape(row_count, heads, HEAD)
    attention = jnp.concatenate([q3[:, j, :] for j in range(heads)], axis=1).astype(jnp.bfloat16)

    def x_at(step):
        return (tp // 4) * 4 + (here + step) % 4

    last = len(X_STEPS)
    scatter = []
    for k, step in enumerate(X_STEPS):
        w_loads[k].wait()
        staged[k] = jnp.dot(attention, held[k], preferred_element_type=jnp.float32).astype(staged.dtype)
        copy = pltpu.make_async_remote_copy(
            src_ref=staged.at[k], dst_ref=parts.at[k], send_sem=rs_send.at[k], recv_sem=rs_recv.at[k],
            device_id=(rep, x_at(step)), device_id_type=MESH,
        )
        copy.start()
        scatter.append(copy)
    issue(PORTIONS[3])
    w_loads[last].wait()
    total = jnp.dot(attention, held[last], preferred_element_type=jnp.float32)
    for k in range(last):
        scatter[k].wait_recv()
        total = total + parts[k].astype(jnp.float32)
    sums[0] = total.astype(sums.dtype)
    swap = pltpu.make_async_remote_copy(
        src_ref=sums.at[0], dst_ref=sums.at[1], send_sem=swap_send, recv_sem=swap_recv,
        device_id=(rep, (tp + 4) % 8), device_id_type=MESH,
    )
    swap.start()
    issue(PORTIONS[4])
    swap.wait_recv()
    columns = pl.ds(pl.multiple_of(here * block, block), block)
    attended[:, columns] = (sums[0].astype(jnp.float32) + sums[1].astype(jnp.float32)).astype(attended.dtype)
    gather = []
    for k, step in enumerate(X_STEPS):
        copy = pltpu.make_async_remote_copy(
            src_ref=attended.at[:, columns], dst_ref=attended.at[:, columns], send_sem=ag_send.at[k], recv_sem=ag_recv.at[k],
            device_id=(rep, x_at(step)), device_id_type=MESH,
        )
        copy.start()
        gather.append(copy)
    issue(len(pieces) * CHUNKS)
    swap.wait_send()
    for copy in pairs_sent:
        copy.wait_send()
    for copy in metas + asks + answers + scatter:
        copy.wait_send()
    for copy in gather + bulk:
        copy.wait()


def run_layer(queries, new_token_kv, resident_cache, resident_lengths, new_caches, new_lengths, handoff, out_weight):
    count, _, half, wide = new_caches.shape
    width = wide // 2
    groups = lax.axis_size("rep")
    entries = groups * CAP
    rows, depth = queries.shape
    heads = depth // HEAD
    tile = CAP * heads
    pairs = rows * heads
    columns = out_weight.shape[1]
    wide_x = len(X_STEPS) + 1
    block = columns // wide_x
    peers, x_peers = len(REP_STEPS), len(X_STEPS)
    kind = new_caches.dtype
    dma = pltpu.SemaphoreType.DMA
    vmem = pl.BlockSpec(memory_space=pltpu.VMEM)
    smem = pl.BlockSpec(memory_space=pltpu.SMEM)
    far = pl.BlockSpec(memory_space=pl.ANY)
    f32 = jnp.float32
    return pl.pallas_call(
        layer_kernel,
        out_shape=(
            jax.ShapeDtypeStruct((rows, columns), kind),
            jax.ShapeDtypeStruct((entries, 2 * half, width), kind),
            jax.ShapeDtypeStruct((8, pairs), jnp.int32),
        ),
        in_specs=[smem, smem, smem, vmem, vmem, far, far, far],
        out_specs=(vmem, far, vmem),
        scratch_shapes=[
            pltpu.VMEM((groups, 1, HEAD), jnp.int32),
            pltpu.VMEM((groups, 1, HEAD), jnp.int32),
            pltpu.VMEM((count, half, width), kind),
            pltpu.VMEM((count, half, width), kind),
            *[pltpu.VMEM((count, half // CHUNKS, width), kind)] * CHUNKS,
            pltpu.VMEM((groups, CAP, half, width), kind),
            pltpu.VMEM((CHUNKS, groups, CAP, half // CHUNKS, width), kind),
            pltpu.VMEM(resident_cache.shape, kind),
            pltpu.VMEM((wide_x, depth, block), kind),
            pltpu.VMEM((rows, heads, HEAD), f32),
            pltpu.VMEM((groups, tile, HEAD), kind),
            pltpu.VMEM((2, groups, tile, HEAD), kind),
            pltpu.VMEM((2, entries, heads, HEAD), f32),
            pltpu.VMEM((count, tile, HEAD), f32),
            pltpu.VMEM((count, tile, HEAD), f32),
            pltpu.VMEM((2, groups, tile, HEAD), kind),
            pltpu.VMEM((2, groups, tile, HEAD), kind),
            pltpu.VMEM((2, groups, 1, HEAD), f32),
            pltpu.VMEM((2, groups, 1, HEAD), f32),
            pltpu.VMEM((entries * heads, pairs), kind),
            pltpu.VMEM((3, pairs, HEAD), f32),
            pltpu.VMEM((x_peers, rows, block), kind),
            pltpu.VMEM((x_peers, rows, block), kind),
            pltpu.VMEM((2, rows, block), kind),
            dma((2,)), dma((CHUNKS,)), dma((CHUNKS,)), dma((CHUNKS + 1, peers)), dma((CHUNKS + 1, peers)), dma((CHUNKS + 1,)),
            dma((peers,)), dma((peers,)),
            dma((2, groups)), dma((2, groups)), dma((2, groups)), dma((2, groups)), dma((2, groups)), dma((2, groups)), dma((RES_PARTS,)), dma((wide_x,)),
            dma((x_peers,)), dma((x_peers,)), dma, dma, dma((x_peers,)), dma((x_peers,)),
        ],
        compiler_params=pltpu.CompilerParams(
            collective_id=0, has_side_effects=True, vmem_limit_bytes=VMEM_BYTES
        ),
        name="layer",
    )(jnp.swapaxes(handoff, 1, 2), new_lengths, resident_lengths, queries, new_token_kv, resident_cache, new_caches, out_weight)


def install_kernel(res_len, own_kv, table, arrived, resident, updated, buf, own_now, notes, note_sem, get, put):
    rows, tokens, width = buf.shape
    heads = table.shape[1] // rows
    capacity = arrived.shape[1]
    step = 16
    fetch = pltpu.make_async_copy(table, notes, note_sem)
    fetch.start()
    own_now[...] = own_kv[...].astype(jnp.float32)
    fetch.wait()

    def entry(r):
        return notes[0, r * heads] - 1

    def get_new(r):
        return pltpu.make_async_copy(arrived.at[entry(r)], buf.at[r, pl.ds(0, capacity), :], get.at[r])

    def get_old(r):
        return pltpu.make_async_copy(resident.at[r], buf.at[r], get.at[r])

    def start(r, carry):
        @pl.when(entry(r) >= 0)
        def _():
            get_new(r).start()

        @pl.when(entry(r) < 0)
        def _():
            get_old(r).start()
        return carry

    lax.fori_loop(0, rows, start, 0)
    at = iota((step, width), 0)

    def patch(r, carry):
        token = own_now[pl.ds(r, 1), :]
        new = entry(r) >= 0
        length = jnp.where(new, notes[1, r * heads], res_len[0, r])
        block = length // step
        here = pl.ds(pl.multiple_of(block * step, step), step)

        @pl.when(new)
        def _():
            get_new(r).wait()
            kept = jnp.where(at < length - block * step, buf[r, here, :].astype(jnp.float32), 0.0)
            buf[r, here, :] = jnp.where(at == length - block * step, token, kept).astype(buf.dtype)

            def clear(i, carry):
                buf[r, pl.ds(pl.multiple_of(i * step, step), step), :] = jnp.zeros((step, width), buf.dtype)
                return carry

            lax.fori_loop(block + 1, tokens // step, clear, 0)

        @pl.when(jnp.logical_not(new))
        def _():
            get_old(r).wait()
            kept = buf[r, here, :].astype(jnp.float32)
            buf[r, here, :] = jnp.where(at == length - block * step, token, kept).astype(buf.dtype)

        pltpu.make_async_copy(buf.at[r], updated.at[r], put.at[r]).start()
        return carry

    lax.fori_loop(0, rows, patch, 0)

    def finish(r, carry):
        pltpu.make_async_copy(buf.at[r], updated.at[r], put.at[r]).wait()
        return carry

    lax.fori_loop(0, rows, finish, 0)


def install(resident_lengths, new_token_kv, table, arrived, resident_cache):
    rows, _, width = resident_cache.shape
    dma = pltpu.SemaphoreType.DMA
    vmem = pl.BlockSpec(memory_space=pltpu.VMEM)
    smem = pl.BlockSpec(memory_space=pltpu.SMEM)
    far = pl.BlockSpec(memory_space=pl.ANY)
    return pl.pallas_call(
        install_kernel,
        out_shape=jax.ShapeDtypeStruct(resident_cache.shape, resident_cache.dtype),
        in_specs=[smem, vmem, far, far, far],
        out_specs=far,
        scratch_shapes=[
            pltpu.VMEM(resident_cache.shape, resident_cache.dtype),
            pltpu.VMEM((rows, width), jnp.float32),
            pltpu.SMEM(table.shape, jnp.int32),
            dma, dma((rows,)), dma((rows,)),
        ],
        compiler_params=pltpu.CompilerParams(vmem_limit_bytes=VMEM_BYTES),
        name="install",
    )(resident_lengths, new_token_kv, table, arrived, resident_cache)


def body(
    queries,
    new_token_kv,
    resident_cache,
    resident_lengths,
    new_caches,
    new_lengths,
    handoff,
    out_weight,
):
    attended, arrived, table = run_layer(
        queries, new_token_kv, resident_cache, resident_lengths, new_caches, new_lengths, handoff, out_weight
    )
    updated = install(resident_lengths, new_token_kv, table, arrived, resident_cache)
    return (attended, updated)


def solution(mesh):
    placed = (
        P("rep", "tp"),
        P("rep", "tp"),
        P("rep", None, "tp"),
        P("rep", None),
        P("rep", "tp", None, None),
        P("rep", None),
        P("rep", None, None),
        P("tp", None),
    )
    return jax.shard_map(
        body,
        mesh=mesh,
        in_specs=placed,
        out_specs=(P("rep", None), P("rep", None, "tp")),
        check_vma=False,
    )
```

time: 99.8 us -> 78.1 us (0.78)
  the two profiles are of different devices: /device:TPU:32 before, /device:TPU:0 now
where the time goes in v3:
time: 78.1 us; the launch traced here: 77.8 us
  Pallas kernels  76.4 us (98%)
  local copies, waits for them, and re-layouts  0.8 us (1%)
    pallas_call x1, Pallas kernels, run_layer(): pl.pallas_call(layer_kernel, out_shape=(jax.ShapeDtypeStruct((rows, colum...  69.1 us
    pallas_call x1, Pallas kernels, install(): pl.pallas_call(install_kernel, out_shape=jax.ShapeDtypeStruct(resident_ca...  7.29 us

profile of v3, /device:TPU:0, one launch (start us, length us, event | category | flops | bytes accessed | tf_op | source)
XLA Modules:
  0.0 77.8 jit_solution(222689164923892596)
XLA Ops:
  0.6 69.1 %layer.1 = (bf16[32,8192]{1,0:T(8,128)(2,1)}, bf16[32,256,256]{2,1,0:T(8,128)(2,1)}, s32[8,256]{1,0:T(8,128)}) custom-call(s32[1,2,16]{2,1,0:T(2,128)} %bitcast.1, s32[1,16]{1,0:T(1,128)} %new_len.1, s32[1,32]{1,0:T(1,128)} %res_len.3, bf16[32,1024]{1,0:T(8,128)(2,1)} %queries.1, bf16[32,256]{1,0:T(8,128)(2,1)} %own_kv.3, bf16[32,384,256]{2,1,0:T(8,128)(2,1)} %resident.3, ...), custom_call_target="tpu_custom_call" | custom-call | tf_op jit(solution)/shard_map/layer/pallas_call | solution.py:402
  69.7 0.0 copy-start
  69.7 7.3 %install.1 = bf16[32,384,256]{2,1,0:T(8,128)(2,1)} custom-call(s32[1,32]{1,0:T(1,128)} %res_len.3, bf16[32,256]{1,0:T(8,128)(2,1)} %own_kv.3, s32[8,256]{1,0:T(8,128)} %get-tuple-element.6.table, bf16[32,256,256]{2,1,0:T(8,128)(2,1)} %get-tuple-element.7.arrived, bf16[32,384,256]{2,1,0:T(8,128)(2,1)} %resident.3), custom_call_target="tpu_custom_call" | custom-call | tf_op jit(solution)/shard_map/install/pallas_call | solution.py:523
  77.0 0.0 copy-done
  77.0 0.8 %copy.11 = bf16[32,8192]{1,0:T(8,128)(2,1)} copy(bf16[32,8192]{1,0:T(8,128)(2,1)S(1)} %copy-done) | data formatting | bytes 1048576
Async XLA Ops:
  69.7 7.3 %copy-start = (bf16[32,8192]{1,0:T(8,128)(2,1)S(1)}, bf16[32,8192]{1,0:T(8,128)(2,1)}, u32[]{:S(2)}) copy-start(bf16[32,8192]{1,0:T(8,128)(2,1)} %get-tuple-element.10) | copy-start | bytes 1572868

commit v4 on v3

--- a/solution.py
+++ b/solution.py
@@ -17,8 +17,9 @@
 RES_PARTS = 4
 VMEM_BYTES = 63 * 2**20
 CHUNKS = 4
-PORTIONS = (32, 32, 24, 20, 10)
+PORTIONS = (28, 32, 24, 20, 24)
 RES_EARLY = 2
+SPLITS = 2
 
 REP_STEPS = [
     (1, 1, 0), (0, 3, 0), (1, 2, 0), (0, 1, 1), (1, 3, 1), (1, 0, 0), (0, 2, 1), (1, 1, 1),
@@ -74,12 +75,13 @@
 
 
 def layer_kernel(
-    hand, new_len, res_len, queries, own_kv, resident, caches, weight,
-    attended, arrived, table,
+    hand_far, new_len_far, res_len_far, queries_far, own_kv_far, resident, caches, weight,
+    attended_far, arrived, table_far,
+    attended, table, hand, new_len, res_len, queries, own_kv,
     meta_send, meta_all, own, theirs, other0, other1, other2, other3, packed, packed2, res, held, q3, query_out, query_in, query_by, acc_by, note_by, part_out, part_in, note_out, note_in,
     selector, rows3, staged, parts, sums,
     own_sem, pair_send, pair_recv, send, recv, stay, meta_s, meta_r, q_s, q_r, p_s, p_r, n_s, n_r, res_sem, load,
-    rs_send, rs_recv, swap_send, swap_recv, ag_send, ag_recv,
+    rs_send, rs_recv, swap_send, swap_recv, ag_send, ag_recv, small_sem, result_sem,
 ):
     rep, tp = lax.axis_index("rep"), lax.axis_index("tp")
     parity = tp % 2
@@ -87,6 +89,13 @@
     count, half, width = own.shape
     row_count = res.shape[0]
     peers = len(REP_STEPS)
+    smalls = []
+    for k, (source, target) in enumerate(
+        ((hand_far, hand), (new_len_far, new_len), (queries_far, queries), (own_kv_far, own_kv), (res_len_far, res_len))
+    ):
+        copy = pltpu.make_async_copy(source, target, small_sem.at[k])
+        copy.start()
+        smalls.append(copy)
     mine = pl.ds(pl.multiple_of(parity * width, width), width)
     away = pl.ds(pl.multiple_of((1 - parity) * width, width), width)
     own_loads = [
@@ -110,6 +119,8 @@
     for step in TP_STEPS:
         pl.semaphore_signal(barrier, inc=1, device_id=(rep, tp_at(tp, step, -1)), device_id_type=MESH)
 
+    for copy in smalls[:2]:
+        copy.wait()
     targets = [hand[0, 0, i] for i in range(count)]
 
     def slot_picks(group):
@@ -193,6 +204,8 @@
     send_chunk()
     issue(PORTIONS[0])
 
+    for copy in smalls[2:]:
+        copy.wait()
     heads = queries.shape[1] // HEAD
     for j in range(heads):
         q3[:, j, :] = queries[:, j * HEAD:(j + 1) * HEAD].astype(jnp.float32)
@@ -308,6 +321,11 @@
     entry_of = (sub // heads + 1).astype(jnp.float32)
     notes = jnp.where(lane == 0, entry_of, jnp.where(lane == 1, (codes // LEN_UNIT).astype(jnp.float32), 0.0))
     table[...] = contract_first(notes.astype(jnp.bfloat16), selector[...])[0:8, :].astype(jnp.int32)
+    results = [
+        pltpu.make_async_copy(table, table_far, result_sem.at[0]),
+        pltpu.make_async_copy(attended, attended_far, result_sem.at[1]),
+    ]
+    results[0].start()
 
     for copy in answers:
         copy.wait_recv()
@@ -336,47 +354,62 @@
         return (tp // 4) * 4 + (here + step) % 4
 
     last = len(X_STEPS)
+    part_width = block // SPLITS
+
+    def share(k, split):
+        at = slice(split * part_width, (split + 1) * part_width)
+        return jnp.dot(attention, held[k, :, at], preferred_element_type=jnp.float32)
+
     scatter = []
-    for k, step in enumerate(X_STEPS):
-        w_loads[k].wait()
-        staged[k] = jnp.dot(attention, held[k], preferred_element_type=jnp.float32).astype(staged.dtype)
-        copy = pltpu.make_async_remote_copy(
-            src_ref=staged.at[k], dst_ref=parts.at[k], send_sem=rs_send.at[k], recv_sem=rs_recv.at[k],
-            device_id=(rep, x_at(step)), device_id_type=MESH,
-        )
-        copy.start()
-        scatter.append(copy)
+    for split in range(SPLITS):
+        for k, step in enumerate(X_STEPS):
+            if split == 0:
+                w_loads[k].wait()
+            staged[split, k] = share(k, split).astype(staged.dtype)
+            copy = pltpu.make_async_remote_copy(
+                src_ref=staged.at[split, k], dst_ref=parts.at[split, k],
+                send_sem=rs_send.at[split, k], recv_sem=rs_recv.at[split, k],
+                device_id=(rep, x_at(step)), device_id_type=MESH,
+            )
+            copy.start()
+            scatter.append(copy)
     issue(PORTIONS[3])
     w_loads[last].wait()
-    total = jnp.dot(attention, held[last], preferred_element_type=jnp.float32)
-    for k in range(last):
-        scatter[k].wait_recv()
-        total = total + parts[k].astype(jnp.float32)
-    sums[0] = total.astype(sums.dtype)
-    swap = pltpu.make_async_remote_copy(
-        src_ref=sums.at[0], dst_ref=sums.at[1], send_sem=swap_send, recv_sem=swap_recv,
-        device_id=(rep, (tp + 4) % 8), device_id_type=MESH,
-    )
-    swap.start()
+    swaps = []
+    for split in range(SPLITS):
+        total = share(last, split)
+        for k in range(last):
+            scatter[split * last + k].wait_recv()
+            total = total + parts[split, k].astype(jnp.float32)
+        sums[split, 0] = total.astype(sums.dtype)
+        copy = pltpu.make_async_remote_copy(
+            src_ref=sums.at[split, 0], dst_ref=sums.at[split, 1], send_sem=swap_send.at[split], recv_sem=swap_recv.at[split],
+            device_id=(rep, (tp + 4) % 8), device_id_type=MESH,
+        )
+        copy.start()
+        swaps.append(copy)
     issue(PORTIONS[4])
-    swap.wait_recv()
-    columns = pl.ds(pl.multiple_of(here * block, block), block)
-    attended[:, columns] = (sums[0].astype(jnp.float32) + sums[1].astype(jnp.float32)).astype(attended.dtype)
     gather = []
-    for k, step in enumerate(X_STEPS):
-        copy = pltpu.make_async_remote_copy(
-            src_ref=attended.at[:, columns], dst_ref=attended.at[:, columns], send_sem=ag_send.at[k], recv_sem=ag_recv.at[k],
-            device_id=(rep, x_at(step)), device_id_type=MESH,
-        )
-        copy.start()
-        gather.append(copy)
+    for split in range(SPLITS):
+        swaps[split].wait_recv()
+        columns = pl.ds(pl.multiple_of(here * block + split * part_width, part_width), part_width)
+        both = sums[split, 0].astype(jnp.float32) + sums[split, 1].astype(jnp.float32)
+        attended[:, columns] = both.astype(attended.dtype)
+        for k, step in enumerate(X_STEPS):
+            copy = pltpu.make_async_remote_copy(
+                src_ref=attended.at[:, columns], dst_ref=attended.at[:, columns],
+                send_sem=ag_send.at[split, k], recv_sem=ag_recv.at[split, k],
+                device_id=(rep, x_at(step)), device_id_type=MESH,
+            )
+            copy.start()
+            gather.append(copy)
     issue(len(pieces) * CHUNKS)
-    swap.wait_send()
-    for copy in pairs_sent:
+    for copy in gather:
+        copy.wait()
+    results[1].start()
+    for copy in pairs_sent + metas + asks + answers + scatter + swaps:
         copy.wait_send()
-    for copy in metas + asks + answers + scatter:
-        copy.wait_send()
-    for copy in gather + bulk:
+    for copy in bulk + results:
         copy.wait()
 
 
@@ -395,8 +428,6 @@
     peers, x_peers = len(REP_STEPS), len(X_STEPS)
     kind = new_caches.dtype
     dma = pltpu.SemaphoreType.DMA
-    vmem = pl.BlockSpec(memory_space=pltpu.VMEM)
-    smem = pl.BlockSpec(memory_space=pltpu.SMEM)
     far = pl.BlockSpec(memory_space=pl.ANY)
     f32 = jnp.float32
     return pl.pallas_call(
@@ -406,9 +437,16 @@
             jax.ShapeDtypeStruct((entries, 2 * half, width), kind),
             jax.ShapeDtypeStruct((8, pairs), jnp.int32),
         ),
-        in_specs=[smem, smem, smem, vmem, vmem, far, far, far],
-        out_specs=(vmem, far, vmem),
+        in_specs=[far] * 8,
+        out_specs=(far, far, far),
         scratch_shapes=[
+            pltpu.VMEM((rows, columns), kind),
+            pltpu.VMEM((8, pairs), jnp.int32),
+            pltpu.SMEM((1, 2, count), jnp.int32),
+            pltpu.SMEM(new_lengths.shape, jnp.int32),
+            pltpu.SMEM(resident_lengths.shape, jnp.int32),
+            pltpu.VMEM(queries.shape, kind),
+            pltpu.VMEM(new_token_kv.shape, kind),
             pltpu.VMEM((groups, 1, HEAD), jnp.int32),
             pltpu.VMEM((groups, 1, HEAD), jnp.int32),
             pltpu.VMEM((count, half, width), kind),
@@ -430,13 +468,14 @@
             pltpu.VMEM((2, groups, 1, HEAD), f32),
             pltpu.VMEM((entries * heads, pairs), kind),
             pltpu.VMEM((3, pairs, HEAD), f32),
-            pltpu.VMEM((x_peers, rows, block), kind),
-            pltpu.VMEM((x_peers, rows, block), kind),
-            pltpu.VMEM((2, rows, block), kind),
+            pltpu.VMEM((SPLITS, x_peers, rows, block // SPLITS), kind),
+            pltpu.VMEM((SPLITS, x_peers, rows, block // SPLITS), kind),
+            pltpu.VMEM((SPLITS, 2, rows, block // SPLITS), kind),
             dma((2,)), dma((CHUNKS,)), dma((CHUNKS,)), dma((CHUNKS + 1, peers)), dma((CHUNKS + 1, peers)), dma((CHUNKS + 1,)),
             dma((peers,)), dma((peers,)),
             dma((2, groups)), dma((2, groups)), dma((2, groups)), dma((2, groups)), dma((2, groups)), dma((2, groups)), dma((RES_PARTS,)), dma((wide_x,)),
-            dma((x_peers,)), dma((x_peers,)), dma, dma, dma((x_peers,)), dma((x_peers,)),
+            dma((SPLITS, x_peers)), dma((SPLITS, x_peers)), dma((SPLITS,)), dma((SPLITS,)), dma((SPLITS, x_peers)), dma((SPLITS, x_peers)),
+            dma((5,)), dma((2,)),
         ],
         compiler_params=pltpu.CompilerParams(
             collective_id=0, has_side_effects=True, vmem_limit_bytes=VMEM_BYTES
@@ -445,15 +484,22 @@
     )(jnp.swapaxes(handoff, 1, 2), new_lengths, resident_lengths, queries, new_token_kv, resident_cache, new_caches, out_weight)
 
 
-def install_kernel(res_len, own_kv, table, arrived, resident, updated, buf, own_now, notes, note_sem, get, put):
+def install_kernel(
+    res_len_far, own_kv_far, table, arrived, resident, attended_in, updated, attended, buf, own_now, notes, res_len, own_kv, whole, small_sem, hand_on, get, put
+):
     rows, tokens, width = buf.shape
     heads = table.shape[1] // rows
     capacity = arrived.shape[1]
     step = 16
-    fetch = pltpu.make_async_copy(table, notes, note_sem)
-    fetch.start()
-    own_now[...] = own_kv[...].astype(jnp.float32)
-    fetch.wait()
+    smalls = []
+    for k, (source, target) in enumerate(((table, notes), (res_len_far, res_len), (own_kv_far, own_kv))):
+        copy = pltpu.make_async_copy(source, target, small_sem.at[k])
+        copy.start()
+        smalls.append(copy)
+    whole_in = pltpu.make_async_copy(attended_in, whole, hand_on.at[0])
+    whole_out = pltpu.make_async_copy(whole, attended, hand_on.at[1])
+    whole_in.start()
+    smalls[0].wait()
 
     def entry(r):
         return notes[0, r * heads] - 1
@@ -468,6 +514,7 @@
         @pl.when(entry(r) >= 0)
         def _():
             get_new(r).start()
+            buf[r, capacity:tokens, :] = jnp.zeros((tokens - capacity, width), buf.dtype)
 
         @pl.when(entry(r) < 0)
         def _():
@@ -475,6 +522,11 @@
         return carry
 
     lax.fori_loop(0, rows, start, 0)
+    for copy in smalls[1:]:
+        copy.wait()
+    own_now[...] = own_kv[...].astype(jnp.float32)
+    whole_in.wait()
+    whole_out.start()
     at = iota((step, width), 0)
 
     def patch(r, carry):
@@ -494,7 +546,7 @@
                 buf[r, pl.ds(pl.multiple_of(i * step, step), step), :] = jnp.zeros((step, width), buf.dtype)
                 return carry
 
-            lax.fori_loop(block + 1, tokens // step, clear, 0)
+            lax.fori_loop(block + 1, capacity // step, clear, 0)
 
         @pl.when(jnp.logical_not(new))
         def _():
@@ -512,28 +564,33 @@
         return carry
 
     lax.fori_loop(0, rows, finish, 0)
-
-
-def install(resident_lengths, new_token_kv, table, arrived, resident_cache):
+    whole_out.wait()
+
+
+def install(resident_lengths, new_token_kv, table, arrived, resident_cache, attended):
     rows, _, width = resident_cache.shape
     dma = pltpu.SemaphoreType.DMA
-    vmem = pl.BlockSpec(memory_space=pltpu.VMEM)
-    smem = pl.BlockSpec(memory_space=pltpu.SMEM)
     far = pl.BlockSpec(memory_space=pl.ANY)
     return pl.pallas_call(
         install_kernel,
-        out_shape=jax.ShapeDtypeStruct(resident_cache.shape, resident_cache.dtype),
-        in_specs=[smem, vmem, far, far, far],
-        out_specs=far,
+        out_shape=(
+            jax.ShapeDtypeStruct(resident_cache.shape, resident_cache.dtype),
+            jax.ShapeDtypeStruct(attended.shape, attended.dtype),
+        ),
+        in_specs=[far] * 6,
+        out_specs=(far, far),
         scratch_shapes=[
             pltpu.VMEM(resident_cache.shape, resident_cache.dtype),
             pltpu.VMEM((rows, width), jnp.float32),
             pltpu.SMEM(table.shape, jnp.int32),
-            dma, dma((rows,)), dma((rows,)),
+            pltpu.SMEM(resident_lengths.shape, jnp.int32),
+            pltpu.VMEM(new_token_kv.shape, new_token_kv.dtype),
+            pltpu.VMEM(attended.shape, attended.dtype),
+            dma((3,)), dma((2,)), dma((rows,)), dma((rows,)),
         ],
         compiler_params=pltpu.CompilerParams(vmem_limit_bytes=VMEM_BYTES),
         name="install",
-    )(resident_lengths, new_token_kv, table, arrived, resident_cache)
+    )(resident_lengths, new_token_kv, table, arrived, resident_cache, attended)
 
 
 def body(
@@ -549,7 +606,7 @@
     attended, arrived, table = run_layer(
         queries, new_token_kv, resident_cache, resident_lengths, new_caches, new_lengths, handoff, out_weight
     )
-    updated = install(resident_lengths, new_token_kv, table, arrived, resident_cache)
+    updated, attended = install(resident_lengths, new_token_kv, table, arrived, resident_cache, attended)
     return (attended, updated)
 
 

time: 78.1 us -> 73.4 us (0.940)
  Pallas kernels: 76.4 us -> 72.1 us
  local copies, waits for them, and re-layouts: 0.8 us -> 0 us
    pallas_call x1, Pallas kernels: 69.1 us -> 65.5 us  [run_layer(): pl.pallas_call(layer_kernel, out_shape=(jax.ShapeDtypeStruct((rows, colum...]
    unnamed x3 -> x0, local copies, waits for them, and re-layouts: 0.8 us -> none
where the time goes in v4:
time: 73.4 us; the launch traced here: 72.7 us
  Pallas kernels  72.1 us (98%)
    pallas_call x1, Pallas kernels, run_layer(): pl.pallas_call(layer_kernel, out_shape=(jax.ShapeDtypeStruct((rows, colum...  65.5 us
    pallas_call x1, Pallas kernels, install(): pl.pallas_call(install_kernel, out_shape=(jax.ShapeDtypeStruct(resident_c...  6.52 us

profile of v4, /device:TPU:0, one launch (start us, length us, event | category | flops | bytes accessed | tf_op | source)
XLA Modules:
  0.0 72.7 jit_solution(13983400687658065811)
XLA Ops:
  0.6 65.5 %layer.1 = (bf16[32,8192]{1,0:T(8,128)(2,1)}, bf16[32,256,256]{2,1,0:T(8,128)(2,1)}, s32[8,256]{1,0:T(8,128)}) custom-call(s32[1,2,16]{2,1,0:T(2,128)} %bitcast.1, s32[1,16]{1,0:T(1,128)} %new_len_far.1, s32[1,32]{1,0:T(1,128)} %res_len_far.3, bf16[32,1024]{1,0:T(8,128)(2,1)} %queries_far.1, bf16[32,256]{1,0:T(8,128)(2,1)} %own_kv_far.3, ...), custom_call_target="tpu_custom_call" | custom-call | tf_op jit(solution)/shard_map/layer/pallas_call | solution.py:433
  66.2 6.5 %install.1 = (bf16[32,384,256]{2,1,0:T(8,128)(2,1)}, bf16[32,8192]{1,0:T(8,128)(2,1)}) custom-call(s32[1,32]{1,0:T(1,128)} %res_len_far.3, bf16[32,256]{1,0:T(8,128)(2,1)} %own_kv_far.3, s32[8,256]{1,0:T(8,128)} %get-tuple-element.7.table, bf16[32,256,256]{2,1,0:T(8,128)(2,1)} %get-tuple-element.8.arrived, bf16[32,384,256]{2,1,0:T(8,128)(2,1)} %resident.3, ...), custom_call_target="tpu_custom_call" | custom-call | tf_op jit(solution)/shard_map/install/pallas_call | solution.py:574

commit v5 on v4

--- a/solution.py
+++ b/solution.py
@@ -19,6 +19,7 @@
 CHUNKS = 4
 PORTIONS = (28, 32, 24, 20, 24)
 RES_EARLY = 2
+EARLY_ROWS = 12
 SPLITS = 2
 
 REP_STEPS = [
@@ -485,7 +486,7 @@
 
 
 def install_kernel(
-    res_len_far, own_kv_far, table, arrived, resident, attended_in, updated, attended, buf, own_now, notes, res_len, own_kv, whole, small_sem, hand_on, get, put
+    res_len_far, own_kv_far, table, arrived, resident, attended_in, updated, attended, buf, alt, own_now, notes, res_len, own_kv, whole, small_sem, hand_on, get, fresh, put
 ):
     rows, tokens, width = buf.shape
     heads = table.shape[1] // rows
@@ -499,13 +500,19 @@
     whole_in = pltpu.make_async_copy(attended_in, whole, hand_on.at[0])
     whole_out = pltpu.make_async_copy(whole, attended, hand_on.at[1])
     whole_in.start()
+
+    def early(r, carry):
+        pltpu.make_async_copy(resident.at[r], buf.at[r], get.at[r]).start()
+        return carry
+
+    lax.fori_loop(0, EARLY_ROWS, early, 0)
     smalls[0].wait()
 
     def entry(r):
         return notes[0, r * heads] - 1
 
     def get_new(r):
-        return pltpu.make_async_copy(arrived.at[entry(r)], buf.at[r, pl.ds(0, capacity), :], get.at[r])
+        return pltpu.make_async_copy(arrived.at[entry(r)], alt.at[r, pl.ds(0, capacity), :], fresh.at[r])
 
     def get_old(r):
         return pltpu.make_async_copy(resident.at[r], buf.at[r], get.at[r])
@@ -514,9 +521,9 @@
         @pl.when(entry(r) >= 0)
         def _():
             get_new(r).start()
-            buf[r, capacity:tokens, :] = jnp.zeros((tokens - capacity, width), buf.dtype)
-
-        @pl.when(entry(r) < 0)
+            alt[r, capacity:tokens, :] = jnp.zeros((tokens - capacity, width), buf.dtype)
+
+        @pl.when((entry(r) < 0) & (r >= EARLY_ROWS))
         def _():
             get_old(r).start()
         return carry
@@ -539,28 +546,34 @@
         @pl.when(new)
         def _():
             get_new(r).wait()
-            kept = jnp.where(at < length - block * step, buf[r, here, :].astype(jnp.float32), 0.0)
-            buf[r, here, :] = jnp.where(at == length - block * step, token, kept).astype(buf.dtype)
+            kept = jnp.where(at < length - block * step, alt[r, here, :].astype(jnp.float32), 0.0)
+            alt[r, here, :] = jnp.where(at == length - block * step, token, kept).astype(buf.dtype)
 
             def clear(i, carry):
-                buf[r, pl.ds(pl.multiple_of(i * step, step), step), :] = jnp.zeros((step, width), buf.dtype)
+                alt[r, pl.ds(pl.multiple_of(i * step, step), step), :] = jnp.zeros((step, width), buf.dtype)
                 return carry
 
             lax.fori_loop(block + 1, capacity // step, clear, 0)
+            pltpu.make_async_copy(alt.at[r], updated.at[r], put.at[r]).start()
 
         @pl.when(jnp.logical_not(new))
         def _():
             get_old(r).wait()
             kept = buf[r, here, :].astype(jnp.float32)
             buf[r, here, :] = jnp.where(at == length - block * step, token, kept).astype(buf.dtype)
-
-        pltpu.make_async_copy(buf.at[r], updated.at[r], put.at[r]).start()
+            pltpu.make_async_copy(buf.at[r], updated.at[r], put.at[r]).start()
+
         return carry
 
     lax.fori_loop(0, rows, patch, 0)
 
     def finish(r, carry):
         pltpu.make_async_copy(buf.at[r], updated.at[r], put.at[r]).wait()
+
+        @pl.when((entry(r) >= 0) & (r < EARLY_ROWS))
+        def _():
+            get_old(r).wait()
+
         return carry
 
     lax.fori_loop(0, rows, finish, 0)
@@ -581,12 +594,13 @@
         out_specs=(far, far),
         scratch_shapes=[
             pltpu.VMEM(resident_cache.shape, resident_cache.dtype),
+            pltpu.VMEM(resident_cache.shape, resident_cache.dtype),
             pltpu.VMEM((rows, width), jnp.float32),
             pltpu.SMEM(table.shape, jnp.int32),
             pltpu.SMEM(resident_lengths.shape, jnp.int32),
             pltpu.VMEM(new_token_kv.shape, new_token_kv.dtype),
             pltpu.VMEM(attended.shape, attended.dtype),
-            dma((3,)), dma((2,)), dma((rows,)), dma((rows,)),
+            dma((3,)), dma((2,)), dma((rows,)), dma((rows,)), dma((rows,)),
         ],
         compiler_params=pltpu.CompilerParams(vmem_limit_bytes=VMEM_BYTES),
         name="install",

time: 73.4 us -> 72.6 us (0.989)
  Pallas kernels: 72.1 us -> 71.1 us
    pallas_call x1, Pallas kernels: 6.52 us -> 5.62 us  [install(): pl.pallas_call(install_kernel, out_shape=(jax.ShapeDtypeStruct(resident_c...]
where the time goes in v5:
time: 72.6 us; the launch traced here: 71.8 us
  Pallas kernels  71.1 us (98%)
    pallas_call x1, Pallas kernels, run_layer(): pl.pallas_call(layer_kernel, out_shape=(jax.ShapeDtypeStruct((rows, colum...  65.5 us
    pallas_call x1, Pallas kernels, install(): pl.pallas_call(install_kernel, out_shape=(jax.ShapeDtypeStruct(resident_c...  5.62 us

profile of v5, /device:TPU:0, one launch (start us, length us, event | category | flops | bytes accessed | tf_op | source)
XLA Modules:
  0.0 71.8 jit_solution(2264883559856530757)
XLA Ops:
  0.6 65.5 %layer.1 = (bf16[32,8192]{1,0:T(8,128)(2,1)}, bf16[32,256,256]{2,1,0:T(8,128)(2,1)}, s32[8,256]{1,0:T(8,128)}) custom-call(s32[1,2,16]{2,1,0:T(2,128)} %bitcast.1, s32[1,16]{1,0:T(1,128)} %new_len_far.1, s32[1,32]{1,0:T(1,128)} %res_len_far.3, bf16[32,1024]{1,0:T(8,128)(2,1)} %queries_far.1, bf16[32,256]{1,0:T(8,128)(2,1)} %own_kv_far.3, ...), custom_call_target="tpu_custom_call" | custom-call | tf_op jit(solution)/shard_map/layer/pallas_call | solution.py:434
  66.2 5.6 %install.1 = (bf16[32,384,256]{2,1,0:T(8,128)(2,1)}, bf16[32,8192]{1,0:T(8,128)(2,1)}) custom-call(s32[1,32]{1,0:T(1,128)} %res_len_far.3, bf16[32,256]{1,0:T(8,128)(2,1)} %own_kv_far.3, s32[8,256]{1,0:T(8,128)} %get-tuple-element.7.table, bf16[32,256,256]{2,1,0:T(8,128)(2,1)} %get-tuple-element.8.arrived, bf16[32,384,256]{2,1,0:T(8,128)(2,1)} %resident.3, ...), custom_call_target="tpu_custom_call" | custom-call | tf_op jit(solution)/shard_map/install/pallas_call | solution.py:587
